TPU v7x, 32 devices: a whole 2x2x4 slice. The times are simulated.
32 devices in a mesh: groups: 2 (over y), pool: 4 (over z), mp: 4 (over x, core).
Axes of the slice: x: 2, y: 2, z: 4, core: 2. Of those that a mesh axis runs over, the one named last changes fastest.
Arguments:
- hidden_states: bfloat16 [128, 8192], P(('groups', 'pool'), 'mp'), parts along dimension 0, may hold values from -6 to 6
- dropout_masks: int32 [8, 128, 8192], P(None, 'groups', 'mp'), parts along dimension 1, may hold values 0 or 1
- gate_weight: bfloat16 [8192, 14784], P('mp', 'pool'), may hold values from -0.0625 to 0.0625
- up_weight: bfloat16 [8192, 14784], P('mp', 'pool'), may hold values from -0.0625 to 0.0625
Outputs:
- activated: bfloat16 [8, 128, 14784], P(None, ('groups', 'mp'), 'pool'), parts along dimension 1
There are 2 independent parts, one for each index of `groups`. A program takes and returns all parts, laid end to end along the dimension named above; an argument that names none is the same for every part. Nothing has to cross between parts.
All inputs are finite; a program needn't handle non-finite values. No bound on the sum of `dropout_masks` on one device may be relied on, other than what follows from the above.
Results may differ from a plain program's by a relative error of at most 0.015.
Values may be sent and summed in bfloat16 or wider, within the bound.
No kernel may reach another device: no remote copies, remote signals or barrier semaphores. Data moves between devices by JAX's collectives and lax.ppermute only.
A program may use at most 128 MiB of HBM per device.

v0:
```python
import jax
import jax.numpy as jnp
from jax import lax
from jax.sharding import PartitionSpec as P


def project_both(masked, gate_weight, up_weight):
    gate = jnp.einsum("mnd,df->mnf", masked, gate_weight, preferred_element_type=jnp.float32)
    up = jnp.einsum("mnd,df->mnf", masked, up_weight, preferred_element_type=jnp.float32)
    return jnp.stack([gate, up], axis=2)


def body(hidden_states, dropout_masks, gate_weight, up_weight):
    tok_local = hidden_states.shape[0]
    offset = lax.axis_index("pool") * tok_local
    local_masks = lax.dynamic_slice_in_dim(dropout_masks, offset, tok_local, 1)
    masked = (
        hidden_states.astype(jnp.float32)[None] * local_masks.astype(jnp.float32) * (1.0 / 0.9)
    ).astype(jnp.bfloat16)
    terms = project_both(lax.all_gather(masked, "pool", axis=1, tiled=True), gate_weight, up_weight)
    summed = lax.psum_scatter(
        terms.astype(jnp.bfloat16), "mp", scatter_dimension=1, tiled=True
    ).astype(jnp.float32)
    return (jax.nn.silu(summed[:, :, 0]) * summed[:, :, 1]).astype(jnp.bfloat16)


def solution(mesh):
    in_specs = (
        P(("groups", "pool"), "mp"),
        P(None, "groups", "mp"),
        P("mp", "pool"),
        P("mp", "pool"),
    )
    out_specs = P(None, ("groups", "mp"), "pool")
    return jax.shard_map(body, mesh=mesh, in_specs=in_specs, out_specs=out_specs, check_vma=False)
```

profile of v0, /device:TPU:0, one launch (start us, length us, event | category | flops | bytes accessed | tf_op | source)
XLA Modules:
  0.0 170.9 jit_solution(2482726343821293235)
XLA Ops:
  6.5 0.0 all-gather.2.cloned.1.call-start
  6.5 0.8 convert_element_type.16
  7.4 2.2 %multiply_convert_fusion = bf16[8,16,2048]{2,1,0:T(8,128)(2,1)} fusion(s32[8,64,2048]{2,1,0:T(8,128)} %param.5, s32[]{:T(128)S(6)} %select_n.3, f32[16,2048]{1,0:T(8,128)S(1)} %convert_element_type.16), kind=kLoop, calls=%fused_computation.13 | loop fusion | flops 1048576 | bytes 1703940 | tf_op jit(solution)/shard_map/convert_element_type | solution.py:19
  9.6 0.0 all-gather.2.cloned.1.call-update
  9.6 0.0 reduce-scatter.2.cloned.1.call-start
  9.6 48.7 %all-gather.2.cloned.1.call-done = bf16[8,64,2048]{2,1,0:T(8,128)(2,1)} async-done(((bf16[8,16,2048]{2,1,0:T(8,128)(2,1)}), bf16[8,64,2048]{2,1,0:T(8,128)(2,1)}) %all-gather.2.cloned.1.call-update) | async-done | bytes 2097168 | tf_op jit(solution)/shard_map/all_gather | solution.py:20
  58.4 0.0 copy-start
  58.4 15.6 %fusion.10 = bf16[8,64,1,3696]{3,1,0,2:T(8,128)(2,1)} fusion(bf16[8,64,2048]{2,1,0:T(8,128)(2,1)} %all-gather.2.cloned.1.call-done, bf16[2048,3696]{0,1:T(8,128)(2,1)} %param.7), kind=kOutput, calls=%fused_computation.7 | convolution fusion | flops 7752966144 | bytes 21020672 | tf_op jit(solution)/shard_map/mnd,df->mnf/dot_general | solution.py:9
  74.0 0.0 copy-done
  74.0 13.6 %fusion.13 = bf16[8,64,1,3696]{3,1,0,2:T(8,128)(2,1)} fusion(bf16[8,64,2048]{2,1,0:T(8,128)(2,1)S(1)} %copy-done, bf16[2048,3696]{0,1:T(8,128)(2,1)} %param.6), kind=kOutput, calls=%fused_computation.8 | convolution fusion | flops 7752966144 | bytes 21020672 | tf_op jit(solution)/shard_map/mnd,df->mnf/dot_general | solution.py:8
  87.6 7.1 %pad_maximum_fusion = bf16[8,64,2,3696]{3,1,0,2:T(8,128)(2,1)} fusion(bf16[8,64,1,3696]{3,1,0,2:T(8,128)(2,1)} %fusion.10, bf16[8,64,1,3696]{3,1,0,2:T(8,128)(2,1)} %fusion.13), kind=kLoop, calls=%fused_computation.4 | loop fusion | flops 3784704 | bytes 15138816 | tf_op jit(solution)/shard_map/stack | solution.py:10
  94.7 0.0 reduce-scatter.2.cloned.1.call-update
  94.7 66.1 %reduce-scatter.2.cloned.1.call-done = bf16[8,16,2,3696]{3,1,0,2:T(8,128)(2,1)} async-done(((bf16[8,64,2,3696]{3,1,0,2:T(8,128)(2,1)}), bf16[8,16,2,3696]{3,1,0,2:T(8,128)(2,1)}) %reduce-scatter.2.cloned.1.call-update) | async-done | bytes 1892368 | tf_op jit(solution)/shard_map/reduce_scatter | solution.py:21
  160.8 1.8 %convert_element_type.19 = f32[8,16,2,3696]{3,1,0,2:T(8,128)S(1)} convert(bf16[8,16,2,3696]{3,1,0,2:T(8,128)(2,1)} %reduce-scatter.2.cloned.1.call-done) | non-fusion elementwise | flops 946176 | bytes 5677056 | tf_op jit(solution)/shard_map/convert_element_type | solution.py:23
  162.6 1.5 fusion.17
Async XLA Ops:
  6.5 51.8 %all-gather.2.cloned.1.call-start = ((), (), s32[]{:S(2)}) async-start(), calls=%async_computation.1 | async-start | bytes 2621440 | tf_op jit(solution)/shard_map/all_gather | solution.py:20
  9.6 151.2 %reduce-scatter.2.cloned.1.call-start = ((), (), s32[]{:S(2)}) async-start(), calls=%async_computation.2 | async-start | bytes 9502720 | tf_op jit(solution)/shard_map/reduce_scatter | solution.py:21
  58.4 15.6 %copy-start = (bf16[8,64,2048]{2,1,0:T(8,128)(2,1)S(1)}, bf16[8,64,2048]{2,1,0:T(8,128)(2,1)}, u32[]{:S(2)}) copy-start(bf16[8,64,2048]{2,1,0:T(8,128)(2,1)} %all-gather.2.cloned.1.call-done) | copy-start | bytes 6291460
Sparse Core Ops, SparseCore 0:
  9.7 48.6 all-gather.1
  94.8 65.9 reduce-scatter.1
where the time goes:
time: 171 us
  waiting for transfers between devices  115 us (67%)
  matrix products  29.2 us (17%)
  between operations  13.4 us (8%)
  other arithmetic  13.3 us (8%)
    reduce_scatter x1, waiting for transfers between devices, body(): lax.psum_scatter(terms.astype(jnp.bfloat16), 'mp', scatter_dimension=1, t...  66.1 us
    all_gather x1, waiting for transfers between devices, body(): lax.all_gather(masked, 'pool', axis=1, tiled=True)  48.7 us
    dot_general x1, matrix products, project_both(): jnp.einsum('mnd,df->mnf', masked, up_weight, preferred_element_type=jnp.f...  15.6 us
    dot_general x1, matrix products, project_both(): jnp.einsum('mnd,df->mnf', masked, gate_weight, preferred_element_type=jnp...  13.6 us
    another operation x1, other arithmetic, project_both(): return jnp.stack([gate, up], axis=2)  7.05 us
  transfers between devices with their start and end apart: 2, of which 2 were waited for; matrix products, arithmetic and copies ran while one was open for 0% of the time, Pallas kernels for 0%

commit v1 on v0

v1 whole, which is shorter than its diff:
```python
import functools

import jax
import jax.numpy as jnp
from jax import lax
from jax.experimental import pallas as pl
from jax.experimental.pallas import tpu as pltpu
from jax.sharding import PartitionSpec as P

BLOCK = 640
SUB = 320
COST = 1000
MIB = 2**20
NT = (((1,), (1,)), ((), ()))


def flags_kernel(dest_ref, masks_ref, flags_ref):
    del dest_ref
    flags_ref[0] = masks_ref[...].astype(jnp.float32).astype(jnp.bfloat16)


def make_flags(dest, masks, n_mp):
    samples, tokens, width = masks.shape
    rows = tokens // n_mp
    return pl.pallas_call(
        flags_kernel,
        grid_spec=pltpu.PrefetchScalarGridSpec(
            num_scalar_prefetch=1,
            grid=(n_mp,),
            in_specs=[pl.BlockSpec((samples, rows, width), lambda r, dest: (0, dest[r], 0))],
            out_specs=pl.BlockSpec((1, samples, rows, width), lambda r, dest: (r, 0, 0, 0)),
        ),
        out_shape=jax.ShapeDtypeStruct((n_mp, samples, rows, width), jnp.bfloat16),
        compiler_params=pltpu.CompilerParams(vmem_limit_bytes=16 * MIB),
        cost_estimate=pl.CostEstimate(flops=COST, bytes_accessed=COST, transcendentals=0),
        name="flags",
    )(dest, masks)


def mask_kernel(dest_ref, place_ref, flags_ref, *refs):
    hidden_refs, masked_ref, scaled = refs[:-2], refs[-2], refs[-1]
    n_pool, piece, _ = scaled.shape
    n_mp, samples, rows, _ = flags_ref.shape
    for d in range(n_pool):
        scaled[d] = hidden_refs[d][...].astype(jnp.float32) * (1.0 / 0.9)
    step = min(rows, piece)
    for r in range(n_mp):
        for low in range(0, rows, step):
            token = dest_ref[r] * rows + low
            slot = lax.rem(place_ref[0] + n_pool - lax.div(token, piece), n_pool)
            inside = pl.multiple_of(lax.rem(token, piece), step)
            part = scaled[slot, pl.ds(inside, step)]
            for m in range(samples):
                flags = flags_ref[r, m, low : low + step].astype(jnp.float32)
                masked_ref[r, m, low : low + step] = (part * flags).astype(jnp.bfloat16)


def make_masked(dest, place, flags, hiddens):
    n_mp, samples, rows, width = flags.shape
    smem = pl.BlockSpec(memory_space=pltpu.SMEM)
    vmem = pl.BlockSpec(memory_space=pltpu.VMEM)
    out = pl.pallas_call(
        mask_kernel,
        in_specs=[smem, smem, vmem] + [vmem] * len(hiddens),
        out_specs=vmem,
        out_shape=jax.ShapeDtypeStruct(flags.shape, jnp.bfloat16),
        scratch_shapes=[pltpu.VMEM((len(hiddens), *hiddens[0].shape), jnp.float32)],
        compiler_params=pltpu.CompilerParams(vmem_limit_bytes=24 * MIB),
        cost_estimate=pl.CostEstimate(flops=COST, bytes_accessed=COST, transcendentals=0),
        name="masked",
    )(dest, place, flags, *hiddens)
    return out.reshape(n_mp * samples * rows, width)


def project_kernel(start, size, masked_ref, gate_ref, up_ref, send_ref, keep_ref, held, sems):
    half = send_ref.shape[2]
    pieces = []
    for low in range(0, size, SUB):
        for which, ref in enumerate((gate_ref, up_ref)):
            n = min(SUB, size - low)
            copy = pltpu.make_async_copy(
                ref.at[pl.ds(start + low, n)], held.at[which, pl.ds(low, n)], sems.at[len(pieces)]
            )
            copy.start()
            pieces.append((which, low, n, copy))
    for which, low, n, copy in pieces:
        copy.wait()
        terms = lax.dot_general(
            held[which, low : low + n], masked_ref[...], NT, preferred_element_type=jnp.float32
        )
        send_ref[which, low : low + n] = terms[:, :half].astype(jnp.bfloat16)
        keep_ref[which, low : low + n] = terms[:, half:].astype(jnp.bfloat16)


def project(masked, gate_t, up_t, start, size):
    rows, width = masked.shape
    out = jax.ShapeDtypeStruct((2, size, rows // 2), jnp.bfloat16)
    return pl.pallas_call(
        functools.partial(project_kernel, start, size),
        in_specs=[pl.BlockSpec(memory_space=pltpu.VMEM)] + [pl.BlockSpec(memory_space=pltpu.HBM)] * 2,
        out_specs=[pl.BlockSpec(memory_space=pltpu.VMEM)] * 2,
        out_shape=[out, out],
        scratch_shapes=[
            pltpu.VMEM((2, size, width), jnp.bfloat16),
            pltpu.SemaphoreType.DMA((2 * pl.cdiv(size, SUB),)),
        ],
        compiler_params=pltpu.CompilerParams(vmem_limit_bytes=50 * MIB),
        cost_estimate=pl.CostEstimate(flops=COST, bytes_accessed=COST, transcendentals=0),
        name=f"project_{start}",
    )(masked, gate_t, up_t)


def swiglu_kernel(n_far, *refs):
    keep_ref, recv_ref, *rest = refs
    far_refs, out_ref = rest[:n_far], rest[-1]
    sums = []
    for which in range(2):
        total = keep_ref[which].astype(jnp.float32) + recv_ref[which].astype(jnp.float32)
        for far in far_refs:
            total = total + far[which].astype(jnp.float32)
        sums.append(total)
    gate, up = sums
    act = jnp.transpose(gate / (1.0 + jnp.exp(-gate)) * up)
    samples, rows, _ = out_ref.shape
    out_ref[...] = act.reshape(samples, rows, act.shape[1]).astype(jnp.bfloat16)


def swiglu(keep, recv, fars, prev, index, samples, rows, hidden_units, block):
    cols = samples * rows
    size = keep.shape[1]
    last = keep.shape[2] // cols - 1
    own = pl.BlockSpec((2, block, cols), lambda i: (0, 0, last))
    far = pl.BlockSpec((2, block, cols), lambda i: (0, 0, 0))
    args = [keep, recv, *fars]
    specs = [own, own] + [far] * len(fars)
    aliases = {}
    if prev is not None:
        aliases = {len(args): 0}
        args.append(prev)
        specs.append(pl.BlockSpec(memory_space=pl.ANY))
    return pl.pallas_call(
        functools.partial(swiglu_kernel, len(fars)),
        grid=(1,),
        in_specs=specs,
        out_specs=pl.BlockSpec((samples, rows, block), lambda i: (0, 0, index)),
        out_shape=jax.ShapeDtypeStruct((samples, rows, hidden_units), jnp.bfloat16),
        input_output_aliases=aliases,
        compiler_params=pltpu.CompilerParams(vmem_limit_bytes=24 * MIB),
        cost_estimate=pl.CostEstimate(flops=COST, bytes_accessed=COST, transcendentals=0),
        name=f"swiglu_{index}",
    )(*args)


def body(n_mp, n_pool, hidden_states, dropout_masks, gate_weight, up_weight):
    samples, tokens, _ = dropout_masks.shape
    units = gate_weight.shape[1]
    rows = tokens // n_mp
    chips = n_mp // 2
    cols = samples * rows
    me = lax.axis_index("mp")
    chip, core = me // 2, me % 2
    offsets = list(range(1, chips)) + [0]
    dest = jnp.stack(
        [lax.rem(chip + o, chips) * 2 + (core + b) % 2 for b in (1, 0) for o in offsets]
    ).astype(jnp.int32)
    to_core = [(i, i ^ 1) for i in range(n_mp)]
    to_chip = {o: [(i, (i // 2 + o) % chips * 2 + i % 2) for i in range(n_mp)] for o in range(1, chips)}

    place = lax.axis_index("pool")[None].astype(jnp.int32)
    hiddens = [hidden_states] + [
        lax.ppermute(hidden_states, "pool", [(i, (i + d) % n_pool) for i in range(n_pool)]) for d in range(1, n_pool)
    ]
    flags = make_flags(dest, dropout_masks, n_mp)
    masked = make_masked(dest, place, flags, hiddens)
    gate_t, up_t = gate_weight.T, up_weight.T
    pad = -units % 16
    if pad:
        gate_t = jnp.pad(gate_t, ((0, pad), (0, 0)))
        up_t = jnp.pad(up_t, ((0, pad), (0, 0)))
    height = units + pad
    n_chunks = pl.cdiv(height, BLOCK)
    order = [n_chunks - 1] + list(range(n_chunks - 1))
    out = None
    waiting = []
    for index in order:
        start = index * BLOCK
        size = min(BLOCK, height - start)
        send, keep = project(masked, gate_t, up_t, start, size)
        recv = lax.ppermute(send, "mp", to_core)
        fars = []
        for i, o in enumerate(offsets[:-1]):
            cut = slice(i * cols, (i + 1) * cols)
            both = keep[:, :, cut].astype(jnp.float32) + recv[:, :, cut].astype(jnp.float32)
            both = both.astype(jnp.bfloat16)
            masked, both = lax.optimization_barrier((masked, both))
            fars.append(lax.ppermute(both, "mp", to_chip[o]))
        waiting.append((keep, recv, fars, index))
    for keep, recv, fars, index in waiting:
        out = swiglu(keep, recv, fars, out, index, samples, rows, units, BLOCK)
    return out


def solution(mesh):
    in_specs = (
        P(("groups", "pool"), "mp"),
        P(None, "groups", "mp"),
        P("mp", "pool"),
        P("mp", "pool"),
    )
    out_specs = P(None, ("groups", "mp"), "pool")
    return jax.shard_map(
        functools.partial(body, mesh.shape["mp"], mesh.shape["pool"]),
        mesh=mesh,
        in_specs=in_specs,
        out_specs=out_specs,
        check_vma=False,
    )
```

time: 171 us -> 97.5 us (0.57)
  waiting for transfers between devices: 115 us -> 41.2 us
  Pallas kernels: 0 us -> 37.2 us
  matrix products: 29.2 us -> 0 us
  starting transfers between devices: 0.04 us -> 16 us
  between operations: 13.4 us -> 0.14 us
  other arithmetic: 13.3 us -> 0.59 us
  local copies, waits for them, and re-layouts: 0.01 us -> 2.19 us
    reduce_scatter x1 -> x0, waiting for transfers between devices: 66.1 us -> none  [body(): lax.psum_scatter(terms.astype(jnp.bfloat16), 'mp', scatter_dimension=1, t...]
    all_gather x1 -> x0, waiting for transfers between devices: 48.7 us -> none  [body(): lax.all_gather(masked, 'pool', axis=1, tiled=True)]
    ppermute x0 -> x15, waiting for transfers between devices: none -> 41.2 us  [the longest x6 31.5 us: body(): fars.append(lax.ppermute(both, 'mp', to_chip[o]))]
    pallas_call x0 -> x14, Pallas kernels: none -> 37.2 us  [the longest x6 29.3 us: project(): pl.pallas_call(functools.partial(project_kernel, start, size), in_specs=[...]
    dot_general x2 -> x0, matrix products: 29.2 us -> none  [the longest x1 15.6 us: project_both(): jnp.einsum('mnd,df->mnf', masked, up_weight, preferred_element_type=jnp.f...]
    ppermute x0 -> x15, starting transfers between devices: none -> 16 us  [the longest x3 7.86 us: body(): lax.ppermute(hidden_states, 'pool', [(i, (i + d) % n_pool) for i in range...]
    another operation x1, other arithmetic: 7.05 us -> 0.08 us  [body(): jnp.stack([lax.rem(chip + o, chips) * 2 + (core + b) % 2 for b in (1, 0)...]
    convert_element_type x4 -> x6, other arithmetic: 6.24 us -> 0.51 us  [body(): both = both.astype(jnp.bfloat16)]
  transfers between devices with their start and end apart: 2 -> 15, of which waited for: 2 -> 11; matrix products, arithmetic and copies ran while one was open for 0% -> 0% of each run, Pallas kernels for 0% -> 6%
where the time goes in v1:
time: 97.5 us; the launch traced here: 97.4 us
  waiting for transfers between devices  41.2 us (42%)
  Pallas kernels  37.2 us (38%)
  starting transfers between devices  16 us (16%)
  local copies, waits for them, and re-layouts  2.19 us (2%)
    ppermute x6, waiting for transfers between devices, body(): fars.append(lax.ppermute(both, 'mp', to_chip[o]))  31.5 us
    pallas_call x6, Pallas kernels, project(): pl.pallas_call(functools.partial(project_kernel, start, size), in_specs=[...  29.3 us
    ppermute x6, waiting for transfers between devices, body(): recv = lax.ppermute(send, 'mp', to_core)  9.7 us
    ppermute x3, starting transfers between devices, body(): lax.ppermute(hidden_states, 'pool', [(i, (i + d) % n_pool) for i in range...  7.86 us
    ppermute x6, starting transfers between devices, body(): fars.append(lax.ppermute(both, 'mp', to_chip[o]))  7.05 us
    pallas_call x6, Pallas kernels, swiglu(): pl.pallas_call(functools.partial(swiglu_kernel, len(fars)), grid=(1,), in...  5.88 us
    unnamed x4, local copies, waits for them, and re-layouts  2.19 us
  transfers between devices with their start and end apart: 15, of which 11 were waited for; matrix products, arithmetic and copies ran while one was open for 0% of the time, Pallas kernels for 6%

profile of v1, /device:TPU:0, one launch (start us, length us, event | category | flops | bytes accessed | tf_op | source)
XLA Modules:
  0.0 97.4 jit_solution(2364966487913260393)
XLA Ops:
  0.0 0.0 copy-start.1
  0.0 4.0 %collective-permute-start.1 = (bf16[16,2048]{1,0:T(8,128)(2,1)}, bf16[16,2048]{1,0:T(8,128)(2,1)S(1)}, u32[]{:S(2)}, u32[]{:S(2)}) collective-permute-start(bf16[16,2048]{1,0:T(8,128)(2,1)} %refs_0_.1), channel_id=1, source_target_pairs={{0,8},{4,12},{8,0},{12,4},{1,9},{5,13},{9,1},{13,5},{2,10},{6,14},... | collective-permute-start | bytes 196616 | tf_op jit(solution)/shard_map/ppermute | solution.py:171
  4.0 1.6 %collective-permute-start = (bf16[16,2048]{1,0:T(8,128)(2,1)}, bf16[16,2048]{1,0:T(8,128)(2,1)S(1)}, u32[]{:S(2)}, u32[]{:S(2)}) collective-permute-start(bf16[16,2048]{1,0:T(8,128)(2,1)} %refs_0_.1), channel_id=1, source_target_pairs={{0,4},{4,8},{8,12},{12,0},{1,5},{5,9},{9,13},{13,1},{2,6},{6,10},{... | collective-permute-start | bytes 196616 | tf_op jit(solution)/shard_map/ppermute | solution.py:171
  5.6 2.2 %collective-permute-start.2 = (bf16[16,2048]{1,0:T(8,128)(2,1)}, bf16[16,2048]{1,0:T(8,128)(2,1)S(1)}, u32[]{:S(2)}, u32[]{:S(2)}) collective-permute-start(bf16[16,2048]{1,0:T(8,128)(2,1)} %refs_0_.1), channel_id=1, source_target_pairs={{0,12},{4,0},{8,4},{12,8},{1,13},{5,1},{9,5},{13,9},{2,14},{6,2},{... | collective-permute-start | bytes 196616 | tf_op jit(solution)/shard_map/ppermute | solution.py:171
  7.9 0.1 pad_add_fusion.dest_ref
  7.9 0.0 copy-start
  7.9 2.2 %copy-done = s32[8,64,2048]{2,1,0:T(8,128)S(1)} copy-done((s32[8,64,2048]{2,1,0:T(8,128)S(1)}, s32[8,64,2048]{2,1,0:T(8,128)}, u32[]{:S(2)}) %copy-start) | copy-done | bytes 4194328
  10.1 1.1 %flags.1.flags_ref = bf16[4,8,16,2048]{3,2,1,0:T(8,128)(2,1)S(1)} custom-call(s32[4]{0:T(128)S(1)} %pad_add_fusion.dest_ref, s32[8,64,2048]{2,1,0:T(8,128)S(1)} %copy-done), custom_call_target="tpu_custom_call" | custom-call | flops 1000 | bytes 1000 | tf_op jit(solution)/shard_map/flags/pallas_call | solution.py:25
  11.3 0.0 collective-permute-done.1.refs_2_
  11.3 0.0 collective-permute-done.refs_1_
  11.3 0.0 collective-permute-done.2.refs_3_
  11.3 0.0 copy-done.1
  11.3 0.9 masked.1
  12.3 4.8 %project_3200.1 = (bf16[2,496,256]{2,1,0:T(8,128)(2,1)S(1)}, bf16[2,496,256]{2,1,0:T(8,128)(2,1)S(1)}) custom-call(bf16[512,2048]{1,0:T(8,128)(2,1)S(1)} %bitcast.8, bf16[3696,2048]{1,0:T(8,128)(2,1)} %bitcast.14, bf16[3696,2048]{1,0:T(8,128)(2,1)} %bitcast.20), custom_call_target="tpu_custom_call" | custom-call | flops 1000 | bytes 1000 | tf_op jit(solution)/shard_map/project_3200/pallas_call | solution.py:98
  17.1 0.1 collective-permute-start.3
  17.2 1.9 %collective-permute-done.3.refs_1_ = bf16[2,496,256]{2,1,0:T(8,128)(2,1)S(1)} collective-permute-done((bf16[2,496,256]{2,1,0:T(8,128)(2,1)S(1)}, bf16[2,496,256]{2,1,0:T(8,128)(2,1)S(1)}, u32[]{:S(2)}, u32[]{:S(2)}) %collective-permute-start.3) | collective-permute-done | bytes 507936 | tf_op jit(solution)/shard_map/ppermute | solution.py:189
  19.0 0.1 add_convert_fusion.5
  19.1 4.9 %project_0.1 = (bf16[2,640,256]{2,1,0:T(8,128)(2,1)S(1)}, bf16[2,640,256]{2,1,0:T(8,128)(2,1)S(1)}) custom-call(bf16[512,2048]{1,0:T(8,128)(2,1)S(1)} %bitcast.9, bf16[3696,2048]{1,0:T(8,128)(2,1)} %bitcast.15, bf16[3696,2048]{1,0:T(8,128)(2,1)} %bitcast.21), custom_call_target="tpu_custom_call" | custom-call | flops 1000 | bytes 1000 | tf_op jit(solution)/shard_map/project_0/pallas_call | solution.py:98
  24.0 0.2 collective-permute-start.4
  24.2 2.0 %collective-permute-done.4.refs_1_ = bf16[2,640,256]{2,1,0:T(8,128)(2,1)S(1)} collective-permute-done((bf16[2,640,256]{2,1,0:T(8,128)(2,1)S(1)}, bf16[2,640,256]{2,1,0:T(8,128)(2,1)S(1)}, u32[]{:S(2)}, u32[]{:S(2)}) %collective-permute-start.4) | collective-permute-done | bytes 655392 | tf_op jit(solution)/shard_map/ppermute | solution.py:189
  26.1 0.1 add_convert_fusion.4
  26.2 4.9 %project_640.1 = (bf16[2,640,256]{2,1,0:T(8,128)(2,1)S(1)}, bf16[2,640,256]{2,1,0:T(8,128)(2,1)S(1)}) custom-call(bf16[512,2048]{1,0:T(8,128)(2,1)S(1)} %bitcast.10, bf16[3696,2048]{1,0:T(8,128)(2,1)} %bitcast.16, bf16[3696,2048]{1,0:T(8,128)(2,1)} %bitcast.22), custom_call_target="tpu_custom_call" | custom-call | flops 1000 | bytes 1000 | tf_op jit(solution)/shard_map/project_640/pallas_call | solution.py:98
  31.1 0.2 collective-permute-start.5
  31.3 2.0 %collective-permute-done.5.refs_1_ = bf16[2,640,256]{2,1,0:T(8,128)(2,1)S(1)} collective-permute-done((bf16[2,640,256]{2,1,0:T(8,128)(2,1)S(1)}, bf16[2,640,256]{2,1,0:T(8,128)(2,1)S(1)}, u32[]{:S(2)}, u32[]{:S(2)}) %collective-permute-start.5) | collective-permute-done | bytes 655392 | tf_op jit(solution)/shard_map/ppermute | solution.py:189
  33.3 0.1 add_convert_fusion.3
  33.3 4.9 %project_1280.1 = (bf16[2,640,256]{2,1,0:T(8,128)(2,1)S(1)}, bf16[2,640,256]{2,1,0:T(8,128)(2,1)S(1)}) custom-call(bf16[512,2048]{1,0:T(8,128)(2,1)S(1)} %bitcast.11, bf16[3696,2048]{1,0:T(8,128)(2,1)} %bitcast.17, bf16[3696,2048]{1,0:T(8,128)(2,1)} %bitcast.23), custom_call_target="tpu_custom_call" | custom-call | flops 1000 | bytes 1000 | tf_op jit(solution)/shard_map/project_1280/pallas_call | solution.py:98
  38.2 0.2 collective-permute-start.6
  38.4 2.0 %collective-permute-done.6.refs_1_ = bf16[2,640,256]{2,1,0:T(8,128)(2,1)S(1)} collective-permute-done((bf16[2,640,256]{2,1,0:T(8,128)(2,1)S(1)}, bf16[2,640,256]{2,1,0:T(8,128)(2,1)S(1)}, u32[]{:S(2)}, u32[]{:S(2)}) %collective-permute-start.6) | collective-permute-done | bytes 655392 | tf_op jit(solution)/shard_map/ppermute | solution.py:189
  40.4 0.1 add_convert_fusion.2
  40.5 5.0 %project_1920.1 = (bf16[2,640,256]{2,1,0:T(8,128)(2,1)S(1)}, bf16[2,640,256]{2,1,0:T(8,128)(2,1)S(1)}) custom-call(bf16[512,2048]{1,0:T(8,128)(2,1)S(1)} %bitcast.12, bf16[3696,2048]{1,0:T(8,128)(2,1)} %bitcast.18, bf16[3696,2048]{1,0:T(8,128)(2,1)} %bitcast.24), custom_call_target="tpu_custom_call" | custom-call | flops 1000 | bytes 1000 | tf_op jit(solution)/shard_map/project_1920/pallas_call | solution.py:98
  45.5 0.2 collective-permute-start.7
  45.7 2.0 %collective-permute-done.7.refs_1_ = bf16[2,640,256]{2,1,0:T(8,128)(2,1)S(1)} collective-permute-done((bf16[2,640,256]{2,1,0:T(8,128)(2,1)S(1)}, bf16[2,640,256]{2,1,0:T(8,128)(2,1)S(1)}, u32[]{:S(2)}, u32[]{:S(2)}) %collective-permute-start.7) | collective-permute-done | bytes 655392 | tf_op jit(solution)/shard_map/ppermute | solution.py:189
  47.7 0.1 add_convert_fusion.1
  47.8 4.9 %project_2560.1 = (bf16[2,640,256]{2,1,0:T(8,128)(2,1)S(1)}, bf16[2,640,256]{2,1,0:T(8,128)(2,1)S(1)}) custom-call(bf16[512,2048]{1,0:T(8,128)(2,1)S(1)} %bitcast.13, bf16[3696,2048]{1,0:T(8,128)(2,1)} %bitcast.19, bf16[3696,2048]{1,0:T(8,128)(2,1)} %bitcast.25), custom_call_target="tpu_custom_call" | custom-call | flops 1000 | bytes 1000 | tf_op jit(solution)/shard_map/project_2560/pallas_call | solution.py:98
  52.6 0.2 collective-permute-start.8
  52.9 1.5 %collective-permute-start.14 = (bf16[2,496,128]{2,1,0:T(8,128)(2,1)S(1)}, bf16[2,496,128]{2,1,0:T(8,128)(2,1)S(1)}, u32[]{:S(2)}, u32[]{:S(2)}) collective-permute-start(bf16[2,496,128]{2,1,0:T(8,128)(2,1)S(1)} %add_convert_fusion.5), channel_id=1, source_target_pairs={{0,2},{1,3},{2,0},{3,1},{4,6},{5,7},{6,4},{7,5},{8,10},{9,11},{10,... | collective-permute-start | bytes 761864 | tf_op jit(solution)/shard_map/ppermute | solution.py:196
  54.4 0.5 collective-permute-start.13
  54.9 1.5 %collective-permute-start.12 = (bf16[2,640,128]{2,1,0:T(8,128)(2,1)S(1)}, bf16[2,640,128]{2,1,0:T(8,128)(2,1)S(1)}, u32[]{:S(2)}, u32[]{:S(2)}) collective-permute-start(bf16[2,640,128]{2,1,0:T(8,128)(2,1)S(1)} %add_convert_fusion.3), channel_id=1, source_target_pairs={{0,2},{1,3},{2,0},{3,1},{4,6},{5,7},{6,4},{7,5},{8,10},{9,11},{10,... | collective-permute-start | bytes 983048 | tf_op jit(solution)/shard_map/ppermute | solution.py:196
  56.4 0.5 collective-permute-start.11
  56.9 0.0 collective-permute-done.8.refs_1_
  56.9 1.5 %collective-permute-start.10 = (bf16[2,640,128]{2,1,0:T(8,128)(2,1)S(1)}, bf16[2,640,128]{2,1,0:T(8,128)(2,1)S(1)}, u32[]{:S(2)}, u32[]{:S(2)}) collective-permute-start(bf16[2,640,128]{2,1,0:T(8,128)(2,1)S(1)} %add_convert_fusion.1), channel_id=1, source_target_pairs={{0,2},{1,3},{2,0},{3,1},{4,6},{5,7},{6,4},{7,5},{8,10},{9,11},{10,... | collective-permute-start | bytes 983048 | tf_op jit(solution)/shard_map/ppermute | solution.py:196
  58.4 0.1 add_convert_fusion
  58.5 3.3 %collective-permute-done.14.refs_2_ = bf16[2,496,128]{2,1,0:T(8,128)(2,1)S(1)} collective-permute-done((bf16[2,496,128]{2,1,0:T(8,128)(2,1)S(1)}, bf16[2,496,128]{2,1,0:T(8,128)(2,1)S(1)}, u32[]{:S(2)}, u32[]{:S(2)}) %collective-permute-start.14) | collective-permute-done | bytes 253984 | tf_op jit(solution)/shard_map/ppermute | solution.py:196
  61.8 1.5 %collective-permute-start.9 = (bf16[2,640,128]{2,1,0:T(8,128)(2,1)S(1)}, bf16[2,640,128]{2,1,0:T(8,128)(2,1)S(1)}, u32[]{:S(2)}, u32[]{:S(2)}) collective-permute-start(bf16[2,640,128]{2,1,0:T(8,128)(2,1)S(1)} %add_convert_fusion), channel_id=1, source_target_pairs={{0,2},{1,3},{2,0},{3,1},{4,6},{5,7},{6,4},{7,5},{8,10},{9,11},{10,... | collective-permute-start | bytes 983048 | tf_op jit(solution)/shard_map/ppermute | solution.py:196
  63.3 1.0 swiglu_5.1.refs_3_
  64.3 4.6 %collective-permute-done.13.refs_2_ = bf16[2,640,128]{2,1,0:T(8,128)(2,1)S(1)} collective-permute-done((bf16[2,640,128]{2,1,0:T(8,128)(2,1)S(1)}, bf16[2,640,128]{2,1,0:T(8,128)(2,1)S(1)}, u32[]{:S(2)}, u32[]{:S(2)}) %collective-permute-start.13) | collective-permute-done | bytes 327712 | tf_op jit(solution)/shard_map/ppermute | solution.py:196
  68.8 1.0 %swiglu_0.1.refs_3_ = bf16[8,16,3696]{2,1,0:T(8,128)(2,1)} custom-call(bf16[2,640,256]{2,1,0:T(8,128)(2,1)S(1)} %get-tuple-element.31.refs_0_, bf16[2,640,256]{2,1,0:T(8,128)(2,1)S(1)} %collective-permute-done.4.refs_1_, bf16[2,640,128]{2,1,0:T(8,128)(2,1)S(1)} %collective-permute-done.13.refs_2_, ...), custom_call_target="tpu_custom_call", output_to_operand_aliasing={{}: (3, {})} | custom-call | flops 1000 | bytes 1000 | tf_op jit(solution)/shard_map/swiglu_0/pallas_call | solution.py:141
  69.8 6.0 %collective-permute-done.12.refs_2_ = bf16[2,640,128]{2,1,0:T(8,128)(2,1)S(1)} collective-permute-done((bf16[2,640,128]{2,1,0:T(8,128)(2,1)S(1)}, bf16[2,640,128]{2,1,0:T(8,128)(2,1)S(1)}, u32[]{:S(2)}, u32[]{:S(2)}) %collective-permute-start.12) | collective-permute-done | bytes 327712 | tf_op jit(solution)/shard_map/ppermute | solution.py:196
  75.9 1.0 %swiglu_1.1.refs_3_ = bf16[8,16,3696]{2,1,0:T(8,128)(2,1)} custom-call(bf16[2,640,256]{2,1,0:T(8,128)(2,1)S(1)} %get-tuple-element.34.refs_0_, bf16[2,640,256]{2,1,0:T(8,128)(2,1)S(1)} %collective-permute-done.5.refs_1_, bf16[2,640,128]{2,1,0:T(8,128)(2,1)S(1)} %collective-permute-done.12.refs_2_, ...), custom_call_target="tpu_custom_call", output_to_operand_aliasing={{}: (3, {})} | custom-call | flops 1000 | bytes 1000 | tf_op jit(solution)/shard_map/swiglu_1/pallas_call | solution.py:141
  76.8 6.0 %collective-permute-done.11.refs_2_ = bf16[2,640,128]{2,1,0:T(8,128)(2,1)S(1)} collective-permute-done((bf16[2,640,128]{2,1,0:T(8,128)(2,1)S(1)}, bf16[2,640,128]{2,1,0:T(8,128)(2,1)S(1)}, u32[]{:S(2)}, u32[]{:S(2)}) %collective-permute-start.11) | collective-permute-done | bytes 327712 | tf_op jit(solution)/shard_map/ppermute | solution.py:196
  82.9 1.0 %swiglu_2.1.refs_3_ = bf16[8,16,3696]{2,1,0:T(8,128)(2,1)} custom-call(bf16[2,640,256]{2,1,0:T(8,128)(2,1)S(1)} %get-tuple-element.37.refs_0_, bf16[2,640,256]{2,1,0:T(8,128)(2,1)S(1)} %collective-permute-done.6.refs_1_, bf16[2,640,128]{2,1,0:T(8,128)(2,1)S(1)} %collective-permute-done.11.refs_2_, ...), custom_call_target="tpu_custom_call", output_to_operand_aliasing={{}: (3, {})} | custom-call | flops 1000 | bytes 1000 | tf_op jit(solution)/shard_map/swiglu_2/pallas_call | solution.py:141
  83.9 6.0 %collective-permute-done.10.refs_2_ = bf16[2,640,128]{2,1,0:T(8,128)(2,1)S(1)} collective-permute-done((bf16[2,640,128]{2,1,0:T(8,128)(2,1)S(1)}, bf16[2,640,128]{2,1,0:T(8,128)(2,1)S(1)}, u32[]{:S(2)}, u32[]{:S(2)}) %collective-permute-start.10) | collective-permute-done | bytes 327712 | tf_op jit(solution)/shard_map/ppermute | solution.py:196
  89.9 1.0 %swiglu_3.1.refs_3_ = bf16[8,16,3696]{2,1,0:T(8,128)(2,1)} custom-call(bf16[2,640,256]{2,1,0:T(8,128)(2,1)S(1)} %get-tuple-element.40.refs_0_, bf16[2,640,256]{2,1,0:T(8,128)(2,1)S(1)} %collective-permute-done.7.refs_1_, bf16[2,640,128]{2,1,0:T(8,128)(2,1)S(1)} %collective-permute-done.10.refs_2_, ...), custom_call_target="tpu_custom_call", output_to_operand_aliasing={{}: (3, {})} | custom-call | flops 1000 | bytes 1000 | tf_op jit(solution)/shard_map/swiglu_3/pallas_call | solution.py:141
  90.9 5.5 %collective-permute-done.9.refs_2_ = bf16[2,640,128]{2,1,0:T(8,128)(2,1)S(1)} collective-permute-done((bf16[2,640,128]{2,1,0:T(8,128)(2,1)S(1)}, bf16[2,640,128]{2,1,0:T(8,128)(2,1)S(1)}, u32[]{:S(2)}, u32[]{:S(2)}) %collective-permute-start.9) | collective-permute-done | bytes 327712 | tf_op jit(solution)/shard_map/ppermute | solution.py:196
  96.4 1.0 %swiglu_4.1 = bf16[8,16,3696]{2,1,0:T(8,128)(2,1)} custom-call(bf16[2,640,256]{2,1,0:T(8,128)(2,1)S(1)} %get-tuple-element.43.refs_0_, bf16[2,640,256]{2,1,0:T(8,128)(2,1)S(1)} %collective-permute-done.8.refs_1_, bf16[2,640,128]{2,1,0:T(8,128)(2,1)S(1)} %collective-permute-done.9.refs_2_, ...), custom_call_target="tpu_custom_call", output_to_operand_aliasing={{}: (3, {})} | custom-call | flops 1000 | bytes 1000 | tf_op jit(solution)/shard_map/swiglu_4/pallas_call | solution.py:141
Async XLA Ops:
  0.0 11.3 %copy-start.1 = (bf16[16,2048]{1,0:T(8,128)(2,1)S(1)}, bf16[16,2048]{1,0:T(8,128)(2,1)}, u32[]{:S(2)}) copy-start(bf16[16,2048]{1,0:T(8,128)(2,1)} %refs_0_.1) | copy-start | bytes 196612
  0.0 11.3 %collective-permute-start.1 = (bf16[16,2048]{1,0:T(8,128)(2,1)}, bf16[16,2048]{1,0:T(8,128)(2,1)S(1)}, u32[]{:S(2)}, u32[]{:S(2)}) collective-permute-start(bf16[16,2048]{1,0:T(8,128)(2,1)} %refs_0_.1), channel_id=1, source_target_pairs={{0,8},{4,12},{8,0},{12,4},{1,9},{5,13},{9,1},{13,5},{2,10},{6,14},... | collective-permute-start | bytes 196616 | tf_op jit(solution)/shard_map/ppermute | solution.py:171
  4.0 7.3 %collective-permute-start = (bf16[16,2048]{1,0:T(8,128)(2,1)}, bf16[16,2048]{1,0:T(8,128)(2,1)S(1)}, u32[]{:S(2)}, u32[]{:S(2)}) collective-permute-start(bf16[16,2048]{1,0:T(8,128)(2,1)} %refs_0_.1), channel_id=1, source_target_pairs={{0,4},{4,8},{8,12},{12,0},{1,5},{5,9},{9,13},{13,1},{2,6},{6,10},{... | collective-permute-start | bytes 196616 | tf_op jit(solution)/shard_map/ppermute | solution.py:171
  5.6 5.7 %collective-permute-start.2 = (bf16[16,2048]{1,0:T(8,128)(2,1)}, bf16[16,2048]{1,0:T(8,128)(2,1)S(1)}, u32[]{:S(2)}, u32[]{:S(2)}) collective-permute-start(bf16[16,2048]{1,0:T(8,128)(2,1)} %refs_0_.1), channel_id=1, source_target_pairs={{0,12},{4,0},{8,4},{12,8},{1,13},{5,1},{9,5},{13,9},{2,14},{6,2},{... | collective-permute-start | bytes 196616 | tf_op jit(solution)/shard_map/ppermute | solution.py:171
  7.9 2.2 %copy-start = (s32[8,64,2048]{2,1,0:T(8,128)S(1)}, s32[8,64,2048]{2,1,0:T(8,128)}, u32[]{:S(2)}) copy-start(s32[8,64,2048]{2,1,0:T(8,128)} %masks_ref.1) | copy-start | bytes 12582916
  17.1 2.0 %collective-permute-start.3 = (bf16[2,496,256]{2,1,0:T(8,128)(2,1)S(1)}, bf16[2,496,256]{2,1,0:T(8,128)(2,1)S(1)}, u32[]{:S(2)}, u32[]{:S(2)}) collective-permute-start(bf16[2,496,256]{2,1,0:T(8,128)(2,1)S(1)} %get-tuple-element.29), channel_id=1, source_target_pairs={{0,1},{1,0},{2,3},{3,2},{4,5},{5,4},{6,7},{7,6},{8,9},{9,8},{10,11... | collective-permute-start | bytes 1523720 | tf_op jit(solution)/shard_map/ppermute | solution.py:189
  24.0 2.2 %collective-permute-start.4 = (bf16[2,640,256]{2,1,0:T(8,128)(2,1)S(1)}, bf16[2,640,256]{2,1,0:T(8,128)(2,1)S(1)}, u32[]{:S(2)}, u32[]{:S(2)}) collective-permute-start(bf16[2,640,256]{2,1,0:T(8,128)(2,1)S(1)} %get-tuple-element.32), channel_id=1, source_target_pairs={{0,1},{1,0},{2,3},{3,2},{4,5},{5,4},{6,7},{7,6},{8,9},{9,8},{10,11... | collective-permute-start | bytes 1966088 | tf_op jit(solution)/shard_map/ppermute | solution.py:189
  31.1 2.2 %collective-permute-start.5 = (bf16[2,640,256]{2,1,0:T(8,128)(2,1)S(1)}, bf16[2,640,256]{2,1,0:T(8,128)(2,1)S(1)}, u32[]{:S(2)}, u32[]{:S(2)}) collective-permute-start(bf16[2,640,256]{2,1,0:T(8,128)(2,1)S(1)} %get-tuple-element.35), channel_id=1, source_target_pairs={{0,1},{1,0},{2,3},{3,2},{4,5},{5,4},{6,7},{7,6},{8,9},{9,8},{10,11... | collective-permute-start | bytes 1966088 | tf_op jit(solution)/shard_map/ppermute | solution.py:189
  38.2 2.2 %collective-permute-start.6 = (bf16[2,640,256]{2,1,0:T(8,128)(2,1)S(1)}, bf16[2,640,256]{2,1,0:T(8,128)(2,1)S(1)}, u32[]{:S(2)}, u32[]{:S(2)}) collective-permute-start(bf16[2,640,256]{2,1,0:T(8,128)(2,1)S(1)} %get-tuple-element.38), channel_id=1, source_target_pairs={{0,1},{1,0},{2,3},{3,2},{4,5},{5,4},{6,7},{7,6},{8,9},{9,8},{10,11... | collective-permute-start | bytes 1966088 | tf_op jit(solution)/shard_map/ppermute | solution.py:189
  45.5 2.2 %collective-permute-start.7 = (bf16[2,640,256]{2,1,0:T(8,128)(2,1)S(1)}, bf16[2,640,256]{2,1,0:T(8,128)(2,1)S(1)}, u32[]{:S(2)}, u32[]{:S(2)}) collective-permute-start(bf16[2,640,256]{2,1,0:T(8,128)(2,1)S(1)} %get-tuple-element.41), channel_id=1, source_target_pairs={{0,1},{1,0},{2,3},{3,2},{4,5},{5,4},{6,7},{7,6},{8,9},{9,8},{10,11... | collective-permute-start | bytes 1966088 | tf_op jit(solution)/shard_map/ppermute | solution.py:189
  52.6 4.3 %collective-permute-start.8 = (bf16[2,640,256]{2,1,0:T(8,128)(2,1)S(1)}, bf16[2,640,256]{2,1,0:T(8,128)(2,1)S(1)}, u32[]{:S(2)}, u32[]{:S(2)}) collective-permute-start(bf16[2,640,256]{2,1,0:T(8,128)(2,1)S(1)} %get-tuple-element.44), channel_id=1, source_target_pairs={{0,1},{1,0},{2,3},{3,2},{4,5},{5,4},{6,7},{7,6},{8,9},{9,8},{10,11... | collective-permute-start | bytes 1966088 | tf_op jit(solution)/shard_map/ppermute | solution.py:189
  52.9 9.0 %collective-permute-start.14 = (bf16[2,496,128]{2,1,0:T(8,128)(2,1)S(1)}, bf16[2,496,128]{2,1,0:T(8,128)(2,1)S(1)}, u32[]{:S(2)}, u32[]{:S(2)}) collective-permute-start(bf16[2,496,128]{2,1,0:T(8,128)(2,1)S(1)} %add_convert_fusion.5), channel_id=1, source_target_pairs={{0,2},{1,3},{2,0},{3,1},{4,6},{5,7},{6,4},{7,5},{8,10},{9,11},{10,... | collective-permute-start | bytes 761864 | tf_op jit(solution)/shard_map/ppermute | solution.py:196
  54.4 14.5 %collective-permute-start.13 = (bf16[2,640,128]{2,1,0:T(8,128)(2,1)S(1)}, bf16[2,640,128]{2,1,0:T(8,128)(2,1)S(1)}, u32[]{:S(2)}, u32[]{:S(2)}) collective-permute-start(bf16[2,640,128]{2,1,0:T(8,128)(2,1)S(1)} %add_convert_fusion.4), channel_id=1, source_target_pairs={{0,2},{1,3},{2,0},{3,1},{4,6},{5,7},{6,4},{7,5},{8,10},{9,11},{10,... | collective-permute-start | bytes 983048 | tf_op jit(solution)/shard_map/ppermute | solution.py:196
  54.9 21.0 %collective-permute-start.12 = (bf16[2,640,128]{2,1,0:T(8,128)(2,1)S(1)}, bf16[2,640,128]{2,1,0:T(8,128)(2,1)S(1)}, u32[]{:S(2)}, u32[]{:S(2)}) collective-permute-start(bf16[2,640,128]{2,1,0:T(8,128)(2,1)S(1)} %add_convert_fusion.3), channel_id=1, source_target_pairs={{0,2},{1,3},{2,0},{3,1},{4,6},{5,7},{6,4},{7,5},{8,10},{9,11},{10,... | collective-permute-start | bytes 983048 | tf_op jit(solution)/shard_map/ppermute | solution.py:196
  56.4 26.5 %collective-permute-start.11 = (bf16[2,640,128]{2,1,0:T(8,128)(2,1)S(1)}, bf16[2,640,128]{2,1,0:T(8,128)(2,1)S(1)}, u32[]{:S(2)}, u32[]{:S(2)}) collective-permute-start(bf16[2,640,128]{2,1,0:T(8,128)(2,1)S(1)} %add_convert_fusion.2), channel_id=1, source_target_pairs={{0,2},{1,3},{2,0},{3,1},{4,6},{5,7},{6,4},{7,5},{8,10},{9,11},{10,... | collective-permute-start | bytes 983048 | tf_op jit(solution)/shard_map/ppermute | solution.py:196
  56.9 33.0 %collective-permute-start.10 = (bf16[2,640,128]{2,1,0:T(8,128)(2,1)S(1)}, bf16[2,640,128]{2,1,0:T(8,128)(2,1)S(1)}, u32[]{:S(2)}, u32[]{:S(2)}) collective-permute-start(bf16[2,640,128]{2,1,0:T(8,128)(2,1)S(1)} %add_convert_fusion.1), channel_id=1, source_target_pairs={{0,2},{1,3},{2,0},{3,1},{4,6},{5,7},{6,4},{7,5},{8,10},{9,11},{10,... | collective-permute-start | bytes 983048 | tf_op jit(solution)/shard_map/ppermute | solution.py:196
  61.8 34.6 %collective-permute-start.9 = (bf16[2,640,128]{2,1,0:T(8,128)(2,1)S(1)}, bf16[2,640,128]{2,1,0:T(8,128)(2,1)S(1)}, u32[]{:S(2)}, u32[]{:S(2)}) collective-permute-start(bf16[2,640,128]{2,1,0:T(8,128)(2,1)S(1)} %add_convert_fusion), channel_id=1, source_target_pairs={{0,2},{1,3},{2,0},{3,1},{4,6},{5,7},{6,4},{7,5},{8,10},{9,11},{10,... | collective-permute-start | bytes 983048 | tf_op jit(solution)/shard_map/ppermute | solution.py:196

commit v2 on v1

v2 whole, which is shorter than its diff:
```python
import functools

import jax
import jax.numpy as jnp
from jax import lax
from jax.experimental import pallas as pl
from jax.experimental.pallas import tpu as pltpu
from jax.sharding import PartitionSpec as P

BLOCK = 640
COST = 1000
LAG = 1
VMEM_MIB = 40
FLAGS_MIB = 50
MIB = 2**20
NT = (((1,), (1,)), ((), ()))


def flags_kernel(dest_ref, masks_ref, flags_ref, raw, sems):
    n_mp, samples, rows, width = raw.shape
    blocks = [
        pltpu.make_async_copy(
            masks_ref.at[:, pl.ds(pl.multiple_of(dest_ref[r] * rows, rows), rows)], raw.at[r], sems.at[r]
        )
        for r in range(n_mp)
    ]
    for block in blocks:
        block.start()
    for r, block in enumerate(blocks):
        block.wait()
        flags = raw[r].astype(jnp.float32).astype(jnp.bfloat16)
        flags_ref[r * samples * rows : (r + 1) * samples * rows] = flags.reshape(samples * rows, width)


def make_flags(dest, masks, n_mp):
    samples, tokens, width = masks.shape
    return pl.pallas_call(
        flags_kernel,
        in_specs=[pl.BlockSpec(memory_space=pltpu.SMEM), pl.BlockSpec(memory_space=pltpu.HBM)],
        out_specs=pl.BlockSpec(memory_space=pltpu.VMEM),
        out_shape=jax.ShapeDtypeStruct((samples * tokens, width), jnp.bfloat16),
        scratch_shapes=[
            pltpu.VMEM((n_mp, samples, tokens // n_mp, width), jnp.int32),
            pltpu.SemaphoreType.DMA((n_mp,)),
        ],
        compiler_params=pltpu.CompilerParams(vmem_limit_bytes=FLAGS_MIB * MIB),
        cost_estimate=pl.CostEstimate(flops=COST, bytes_accessed=COST, transcendentals=0),
        name="flags",
    )(dest, masks)


def half_of(size):
    return pl.cdiv(size, 32) * 16


def load(start, size, gate_ref, up_ref, weights_ref, sems):
    bounds = (0, half_of(size), size)
    copies = []
    for piece in range(2):
        low, n = bounds[piece], bounds[piece + 1] - bounds[piece]
        for which, ref in enumerate((gate_ref, up_ref)):
            if n:
                copy = pltpu.make_async_copy(
                    ref.at[pl.ds(start + low, n)], weights_ref.at[which, pl.ds(low, n)], sems.at[which, piece]
                )
                copy.start()
                copies.append(copy)
    return copies


def multiply(part, weights_ref, masked_ref, out_refs):
    far_gate, far_up, near, keep_far, keep_near = out_refs
    far = far_gate.shape[1]
    half = masked_ref.shape[0] // 2
    for which, send_far in enumerate((far_gate, far_up)):
        terms = lax.dot_general(
            weights_ref[which, part], masked_ref[...], NT, preferred_element_type=jnp.float32
        ).astype(jnp.bfloat16)
        send_far[part] = terms[:, :far]
        near[which, part] = terms[:, far:half]
        keep_far[which, part] = terms[:, half : half + far]
        keep_near[which, part] = terms[:, half + far :]


def peer(n_pool, place, d):
    return place ^ d if n_pool & (n_pool - 1) == 0 else (place + d) % n_pool


def slot_of(n_pool, place, owner):
    if n_pool & (n_pool - 1) == 0:
        return lax.bitwise_xor(place, owner)
    return lax.rem(place + n_pool - owner, n_pool)


def first_kernel(now, later, samples, n_mp, dest_ref, place_ref, gate_ref, up_ref, flags_ref, *refs):
    n_pool = len(refs) - (11 if later else 9)
    hidden_refs, refs = refs[:n_pool], refs[n_pool:]
    masked_ref, *refs = refs
    out_refs, refs = refs[:5], refs[5:]
    if later:
        later_ref, scaled, weights, sems, later_sems = refs
    else:
        scaled, weights, sems = refs
    copies = load(*now, gate_ref, up_ref, weights, sems)
    later_copies = load(*later, gate_ref, up_ref, later_ref, later_sems) if later else []
    piece = scaled.shape[1]
    rows = flags_ref.shape[0] // (n_mp * samples)
    for d in range(n_pool):
        scaled[d] = hidden_refs[d][...].astype(jnp.float32) * (1.0 / 0.9)
    step = min(rows, piece)

    @pl.loop(0, n_mp)
    def _(r):
        for low in range(0, rows, step):
            token = dest_ref[r] * rows + low
            slot = slot_of(n_pool, place_ref[0], lax.div(token, piece))
            inside = pl.multiple_of(lax.rem(token, piece), step)
            part = scaled[slot, pl.ds(inside, step)]
            for m in range(samples):
                at = pl.ds(pl.multiple_of((r * samples + m) * rows + low, step), step)
                masked_ref[at] = (part * flags_ref[at].astype(jnp.float32)).astype(jnp.bfloat16)

    size = now[1]
    low = 0
    while copies:
        pair, copies = copies[:2], copies[2:]
        for copy in pair:
            copy.wait()
        high = half_of(size) if copies else size
        multiply(slice(low, high), weights, masked_ref, out_refs)
        low = high
    for copy in later_copies:
        copy.wait()


def product_shapes(rows, size, cols):
    far = rows // 2 - cols
    shapes = [(size, far), (size, far), (2, size, cols), (2, size, far), (2, size, cols)]
    return [jax.ShapeDtypeStruct(shape, jnp.bfloat16) for shape in shapes]


def project_first(dest, place, gate_t, up_t, flags, hiddens, now, later, samples, n_mp, cols):
    rows, width = flags.shape
    smem = pl.BlockSpec(memory_space=pltpu.SMEM)
    vmem = pl.BlockSpec(memory_space=pltpu.VMEM)
    hbm = pl.BlockSpec(memory_space=pltpu.HBM)
    shapes = [jax.ShapeDtypeStruct((rows, width), jnp.bfloat16)] + product_shapes(rows, now[1], cols)
    scratch = [
        pltpu.VMEM((len(hiddens), *hiddens[0].shape), jnp.float32),
        pltpu.VMEM((2, now[1], width), jnp.bfloat16),
        pltpu.SemaphoreType.DMA((2, 2)),
    ]
    if later:
        shapes.append(jax.ShapeDtypeStruct((2, later[1], width), jnp.bfloat16))
        scratch.append(pltpu.SemaphoreType.DMA((2, 2)))
    return pl.pallas_call(
        functools.partial(first_kernel, now, later, samples, n_mp),
        in_specs=[smem, smem, hbm, hbm] + [vmem] * (1 + len(hiddens)),
        out_specs=[vmem] * len(shapes),
        out_shape=shapes,
        scratch_shapes=scratch,
        compiler_params=pltpu.CompilerParams(vmem_limit_bytes=VMEM_MIB * MIB),
        cost_estimate=pl.CostEstimate(flops=COST, bytes_accessed=COST, transcendentals=0),
        name="project_first",
    )(dest, place, gate_t, up_t, flags, *hiddens)


def project_kernel(later, masked_ref, weights_ref, gate_ref, up_ref, *refs):
    out_refs, rest = refs[:5], refs[5:]
    copies = load(*later, gate_ref, up_ref, *rest) if later else []
    size = weights_ref.shape[1]
    step = half_of(size)

    @pl.loop(0, 2)
    def _(i):
        multiply(pl.ds(pl.multiple_of(i * (size - step), 16), step), weights_ref, masked_ref, out_refs)

    for copy in copies:
        copy.wait()


def project(masked, weights, gate_t, up_t, later, cols):
    rows, width = masked.shape
    size = weights.shape[1]
    shapes = product_shapes(rows, size, cols)
    scratch = []
    if later:
        shapes.append(jax.ShapeDtypeStruct((2, later[1], width), jnp.bfloat16))
        scratch.append(pltpu.SemaphoreType.DMA((2, 2)))
    vmem = pl.BlockSpec(memory_space=pltpu.VMEM)
    hbm = pl.BlockSpec(memory_space=pltpu.HBM)
    return pl.pallas_call(
        functools.partial(project_kernel, later),
        in_specs=[vmem, vmem, hbm, hbm],
        out_specs=[vmem] * len(shapes),
        out_shape=shapes,
        scratch_shapes=scratch,
        compiler_params=pltpu.CompilerParams(vmem_limit_bytes=VMEM_MIB * MIB),
        cost_estimate=pl.CostEstimate(flops=COST, bytes_accessed=COST, transcendentals=0),
        name=f"project_{size}",
    )(masked, weights, gate_t, up_t)


def add_kernel(keep_ref, gate_ref, up_ref, *outs):
    cols = outs[0].shape[2]
    for which, ref in enumerate((gate_ref, up_ref)):
        for i, out in enumerate(outs):
            cut = slice(i * cols, (i + 1) * cols)
            total = keep_ref[which, :, cut].astype(jnp.float32) + ref[:, cut].astype(jnp.float32)
            out[which] = total.astype(jnp.bfloat16)


def add_cores(keep, gate, up, cols, name):
    _, size, far = keep.shape
    n = far // cols
    vmem = pl.BlockSpec(memory_space=pltpu.VMEM)
    return pl.pallas_call(
        add_kernel,
        in_specs=[vmem] * 3,
        out_specs=[vmem] * n,
        out_shape=[jax.ShapeDtypeStruct((2, size, cols), jnp.bfloat16)] * n,
        compiler_params=pltpu.CompilerParams(vmem_limit_bytes=16 * MIB),
        cost_estimate=pl.CostEstimate(flops=COST, bytes_accessed=COST, transcendentals=0),
        name=name,
    )(keep, gate, up)


def swiglu_kernel(n_far, *refs):
    keep_ref, recv_ref, *rest = refs
    far_refs, out_ref = rest[:n_far], rest[-1]
    sums = []
    for which in range(2):
        total = keep_ref[which].astype(jnp.float32) + recv_ref[which].astype(jnp.float32)
        for far in far_refs:
            total = total + far[which].astype(jnp.float32)
        sums.append(total)
    gate, up = sums
    act = jnp.transpose(gate / (1.0 + jnp.exp(-gate)) * up)
    samples, rows, _ = out_ref.shape
    out_ref[...] = act.reshape(samples, rows, act.shape[1]).astype(jnp.bfloat16)


def swiglu(keep, recv, fars, prev, index, samples, rows, hidden_units, block):
    cols = samples * rows
    size = keep.shape[1]
    args = [keep, recv, *fars]
    specs = [pl.BlockSpec((2, block, cols), lambda i: (0, 0, 0))] * len(args)
    aliases = {}
    if prev is not None:
        aliases = {len(args): 0}
        args.append(prev)
        specs.append(pl.BlockSpec(memory_space=pl.ANY))
    return pl.pallas_call(
        functools.partial(swiglu_kernel, len(fars)),
        grid=(1,),
        in_specs=specs,
        out_specs=pl.BlockSpec((samples, rows, block), lambda i: (0, 0, index)),
        out_shape=jax.ShapeDtypeStruct((samples, rows, hidden_units), jnp.bfloat16),
        input_output_aliases=aliases,
        compiler_params=pltpu.CompilerParams(vmem_limit_bytes=24 * MIB),
        cost_estimate=pl.CostEstimate(flops=COST, bytes_accessed=COST, transcendentals=0),
        name=f"swiglu_{index}",
    )(*args)


def body(n_mp, n_pool, hidden_states, dropout_masks, gate_weight, up_weight):
    samples, tokens, _ = dropout_masks.shape
    units = gate_weight.shape[1]
    rows = tokens // n_mp
    chips = n_mp // 2
    cols = samples * rows
    me = lax.axis_index("mp")
    chip, core = me // 2, me % 2
    offsets = list(range(1, chips)) + [0]
    dest = jnp.stack(
        [lax.rem(chip + o, chips) * 2 + (core + b) % 2 for b in (1, 0) for o in offsets]
    ).astype(jnp.int32)
    to_core = [(i, i ^ 1) for i in range(n_mp)]
    to_chip = {o: [(i, (i // 2 + o) % chips * 2 + i % 2) for i in range(n_mp)] for o in range(1, chips)}

    place = lax.axis_index("pool")[None].astype(jnp.int32)
    hiddens = [hidden_states] + [
        lax.ppermute(hidden_states, "pool", [(i, peer(n_pool, i, d)) for i in range(n_pool)]) for d in range(1, n_pool)
    ]
    gate_t, up_t = gate_weight.T, up_weight.T
    pad = -units % 16
    if pad:
        gate_t = jnp.pad(gate_t, ((0, pad), (0, 0)))
        up_t = jnp.pad(up_t, ((0, pad), (0, 0)))
    height = units + pad
    n_chunks = pl.cdiv(height, BLOCK)
    order = [n_chunks - 1] + list(range(n_chunks - 1))
    spans = [(index * BLOCK, min(BLOCK, height - index * BLOCK)) for index in order]
    flags = make_flags(dest, dropout_masks, n_mp)
    out = None
    waiting = []
    for i, index in enumerate(order):
        start = spans[i][0]
        later = spans[i + 1] if i + 1 < n_chunks else None
        if i == 0:
            masked, *products = project_first(
                dest, place, gate_t, up_t, flags, hiddens, spans[0], later, samples, n_mp, cols
            )
        else:
            products = project(masked, weights, gate_t, up_t, later, cols)
        far_gate, far_up, near, keep_far, keep_near, *weights = products
        weights = weights[0] if weights else None
        far_gate = lax.ppermute(far_gate, "mp", to_core)
        far_up = lax.ppermute(far_up, "mp", to_core)
        if waiting and later is None:
            near, waiting[-1][2] = lax.optimization_barrier((near, waiting[-1][2]))
        near = lax.ppermute(near, "mp", to_core)
        sums = add_cores(keep_far, far_gate, far_up, cols, f"add_{start}")
        masked, sums = lax.optimization_barrier((masked, sums))
        fars = [lax.ppermute(total, "mp", to_chip[o]) for total, o in zip(sums, offsets)]
        waiting.append([keep_near, near, fars, index])
        if len(waiting) > LAG:
            old = waiting[-1 - LAG]
            masked, old[2] = lax.optimization_barrier((masked, old[2]))
    for keep, recv, fars, index in waiting:
        out = swiglu(keep, recv, fars, out, index, samples, rows, units, BLOCK)
    return out


def solution(mesh):
    in_specs = (
        P(("groups", "pool"), "mp"),
        P(None, "groups", "mp"),
        P("mp", "pool"),
        P("mp", "pool"),
    )
    out_specs = P(None, ("groups", "mp"), "pool")
    return jax.shard_map(
        functools.partial(body, mesh.shape["mp"], mesh.shape["pool"]),
        mesh=mesh,
        in_specs=in_specs,
        out_specs=out_specs,
        check_vma=False,
    )
```

time: 97.5 us -> 68.4 us (0.70)
  waiting for transfers between devices: 41.2 us -> 21.2 us
  Pallas kernels: 37.2 us -> 29.7 us
  local copies, waits for them, and re-layouts: 2.19 us -> 0.01 us
  starting transfers between devices: 16 us -> 17.1 us
    ppermute x15 -> x27, waiting for transfers between devices: 41.2 us -> 21.2 us  [the longest x6 11.3 us: body(): lax.ppermute(total, 'mp', to_chip[o])]
    pallas_call x8 -> x13, Pallas kernels: 31.4 us -> 24.1 us  [the longest x5 15.7 us: project(): pl.pallas_call(functools.partial(project_kernel, later), in_specs=[vmem,...]
    unnamed x4 -> x2, local copies, waits for them, and re-layouts: 2.19 us -> 0.01 us
    ppermute x15 -> x27, starting transfers between devices: 16 us -> 17.1 us  [the longest x6 6.92 us: body(): lax.ppermute(total, 'mp', to_chip[o])]
  transfers between devices with their start and end apart: 15 -> 27, of which waited for: 11 -> 19; matrix products, arithmetic and copies ran while one was open for 0% -> 0% of each run, Pallas kernels for 6% -> 35%
where the time goes in v2:
time: 68.4 us; the launch traced here: 68.2 us
  Pallas kernels  29.7 us (43%)
  waiting for transfers between devices  21.2 us (31%)
  starting transfers between devices  17.1 us (25%)
    pallas_call x5, Pallas kernels, project(): pl.pallas_call(functools.partial(project_kernel, later), in_specs=[vmem,...  15.7 us
    ppermute x6, waiting for transfers between devices, body(): lax.ppermute(total, 'mp', to_chip[o])  11.3 us
    ppermute x6, starting transfers between devices, body(): lax.ppermute(total, 'mp', to_chip[o])  6.92 us
    ppermute x3, starting transfers between devices, body(): lax.ppermute(hidden_states, 'pool', [(i, peer(n_pool, i, d)) for i in ran...  5.62 us
    pallas_call x6, Pallas kernels, swiglu(): pl.pallas_call(functools.partial(swiglu_kernel, len(fars)), grid=(1,), in...  5.61 us
    ppermute x6, waiting for transfers between devices, body(): far_gate = lax.ppermute(far_gate, 'mp', to_core)  5.25 us
    pallas_call x1, Pallas kernels, project_first(): pl.pallas_call(functools.partial(first_kernel, now, later, samples, n_mp)...  5.18 us
    ppermute x3, waiting for transfers between devices, body(): lax.ppermute(hidden_states, 'pool', [(i, peer(n_pool, i, d)) for i in ran...  3.36 us
  transfers between devices with their start and end apart: 27, of which 19 were waited for; matrix products, arithmetic and copies ran while one was open for 0% of the time, Pallas kernels for 35%

profile of v2, /device:TPU:0, one launch (start us, length us, event | category | flops | bytes accessed | tf_op | source)
XLA Modules:
  0.0 68.2 jit_solution(11287551531614092023)
XLA Ops:
  0.0 4.0 %collective-permute-start.1 = (bf16[16,2048]{1,0:T(8,128)(2,1)}, bf16[16,2048]{1,0:T(8,128)(2,1)S(1)}, u32[]{:S(2)}, u32[]{:S(2)}) collective-permute-start(bf16[16,2048]{1,0:T(8,128)(2,1)} %refs_0_.1), channel_id=1, source_target_pairs={{0,8},{4,12},{8,0},{12,4},{1,9},{5,13},{9,1},{13,5},{2,10},{6,14},... | collective-permute-start | bytes 196616 | tf_op jit(solution)/shard_map/ppermute | solution.py:283
  4.0 1.6 %collective-permute-start = (bf16[16,2048]{1,0:T(8,128)(2,1)}, bf16[16,2048]{1,0:T(8,128)(2,1)S(1)}, u32[]{:S(2)}, u32[]{:S(2)}) collective-permute-start(bf16[16,2048]{1,0:T(8,128)(2,1)} %refs_0_.1), channel_id=1, source_target_pairs={{0,4},{4,0},{8,12},{12,8},{1,5},{5,1},{9,13},{13,9},{2,6},{6,2},{1... | collective-permute-start | bytes 196616 | tf_op jit(solution)/shard_map/ppermute | solution.py:283
  5.6 0.0 collective-permute-start.2
  5.6 0.1 pad_add_fusion.dest_ref
  5.7 2.8 %flags.1.flags_ref = bf16[512,2048]{1,0:T(8,128)(2,1)S(1)} custom-call(s32[4]{0:T(128)S(1)} %pad_add_fusion.dest_ref, s32[8,64,2048]{2,1,0:T(8,128)} %masks_ref.1), custom_call_target="tpu_custom_call" | custom-call | flops 1000 | bytes 1000 | tf_op jit(solution)/shard_map/flags/pallas_call | solution.py:37
  8.5 3.4 %collective-permute-done.2.refs_3_ = bf16[16,2048]{1,0:T(8,128)(2,1)S(1)} collective-permute-done((bf16[16,2048]{1,0:T(8,128)(2,1)}, bf16[16,2048]{1,0:T(8,128)(2,1)S(1)}, u32[]{:S(2)}, u32[]{:S(2)}) %collective-permute-start.2) | collective-permute-done | bytes 65568 | tf_op jit(solution)/shard_map/ppermute | solution.py:283
  11.9 5.2 %project_first.1 = (bf16[512,2048]{1,0:T(8,128)(2,1)S(1)}, bf16[496,128]{1,0:T(8,128)(2,1)S(1)}, bf16[496,128]{1,0:T(8,128)(2,1)S(1)}, bf16[2,496,128]{2,1,0:T(8...) custom-call(s32[4]{0:T(128)S(1)} %pad_add_fusion.dest_ref, ...), custom_call_target="tpu_custom_call" | custom-call | flops 1000 | bytes 1000 | tf_op jit(solution)/shard_map/project_first/pallas_call | solution.py:156
  17.1 0.1 collective-permute-start.3
  17.2 0.5 collective-permute-start.4
  17.7 0.8 %collective-permute-done.3.gate_ref = bf16[496,128]{1,0:T(8,128)(2,1)S(1)} collective-permute-done((bf16[496,128]{1,0:T(8,128)(2,1)S(1)}, bf16[496,128]{1,0:T(8,128)(2,1)S(1)}, u32[]{:S(2)}, u32[]{:S(2)}) %collective-permute-start.3) | collective-permute-done | bytes 127008 | tf_op jit(solution)/shard_map/ppermute | solution.py:308
  18.5 0.2 collective-permute-done.4.up_ref
  18.7 0.1 add_3200.1
  18.7 1.6 %collective-permute-start.7 = (bf16[2,496,128]{2,1,0:T(8,128)(2,1)S(1)}, bf16[2,496,128]{2,1,0:T(8,128)(2,1)S(1)}, u32[]{:S(2)}, u32[]{:S(2)}) collective-permute-start(bf16[2,496,128]{2,1,0:T(8,128)(2,1)S(1)} %add_3200.1), channel_id=1, source_target_pairs={{0,2},{1,3},{2,0},{3,1},{4,6},{5,7},{6,4},{7,5},{8,10},{9,11},{10,... | collective-permute-start | bytes 761864 | tf_op jit(solution)/shard_map/ppermute | solution.py:315
  20.3 3.1 %project_640.5 = (bf16[640,128]{1,0:T(8,128)(2,1)S(1)}, bf16[640,128]{1,0:T(8,128)(2,1)S(1)}, bf16[2,640,128]{2,1,0:T(8,128)(2,1)S(1)}, bf16[2,640,128]{2,1,0:T(...) custom-call(bf16[512,2048]{1,0:T(8,128)(2,1)S(1)} %get-tuple-element.94.masked_ref, ...), custom_call_target="tpu_custom_call" | custom-call | flops 1000 | bytes 1000 | tf_op jit(solution)/shard_map/project_640/pallas_call | solution.py:192
  23.4 0.1 collective-permute-start.5
  23.6 0.5 collective-permute-start.6
  24.0 0.9 %collective-permute-done.5.gate_ref = bf16[640,128]{1,0:T(8,128)(2,1)S(1)} collective-permute-done((bf16[640,128]{1,0:T(8,128)(2,1)S(1)}, bf16[640,128]{1,0:T(8,128)(2,1)S(1)}, u32[]{:S(2)}, u32[]{:S(2)}) %collective-permute-start.5) | collective-permute-done | bytes 163872 | tf_op jit(solution)/shard_map/ppermute | solution.py:308
  24.9 0.2 collective-permute-done.6.up_ref
  25.1 0.1 add_0.1
  25.2 0.6 collective-permute-start.10
  25.8 1.3 %collective-permute-done.7.refs_2_ = bf16[2,496,128]{2,1,0:T(8,128)(2,1)S(1)} collective-permute-done((bf16[2,496,128]{2,1,0:T(8,128)(2,1)S(1)}, bf16[2,496,128]{2,1,0:T(8,128)(2,1)S(1)}, u32[]{:S(2)}, u32[]{:S(2)}) %collective-permute-start.7) | collective-permute-done | bytes 253984 | tf_op jit(solution)/shard_map/ppermute | solution.py:315
  27.2 3.1 %project_640.6 = (bf16[640,128]{1,0:T(8,128)(2,1)S(1)}, bf16[640,128]{1,0:T(8,128)(2,1)S(1)}, bf16[2,640,128]{2,1,0:T(8,128)(2,1)S(1)}, bf16[2,640,128]{2,1,0:T(...) custom-call(bf16[512,2048]{1,0:T(8,128)(2,1)S(1)} %get-tuple-element.94.masked_ref, ...), custom_call_target="tpu_custom_call" | custom-call | flops 1000 | bytes 1000 | tf_op jit(solution)/shard_map/project_640/pallas_call | solution.py:192
  30.3 0.1 collective-permute-start.8
  30.4 0.5 collective-permute-start.9
  30.9 0.9 %collective-permute-done.8.gate_ref = bf16[640,128]{1,0:T(8,128)(2,1)S(1)} collective-permute-done((bf16[640,128]{1,0:T(8,128)(2,1)S(1)}, bf16[640,128]{1,0:T(8,128)(2,1)S(1)}, u32[]{:S(2)}, u32[]{:S(2)}) %collective-permute-start.8) | collective-permute-done | bytes 163872 | tf_op jit(solution)/shard_map/ppermute | solution.py:308
  31.8 0.2 collective-permute-done.9.up_ref
  32.0 0.1 add_640.1
  32.1 1.6 %collective-permute-start.13 = (bf16[2,640,128]{2,1,0:T(8,128)(2,1)S(1)}, bf16[2,640,128]{2,1,0:T(8,128)(2,1)S(1)}, u32[]{:S(2)}, u32[]{:S(2)}) collective-permute-start(bf16[2,640,128]{2,1,0:T(8,128)(2,1)S(1)} %add_640.1), channel_id=1, source_target_pairs={{0,2},{1,3},{2,0},{3,1},{4,6},{5,7},{6,4},{7,5},{8,10},{9,11},{10,... | collective-permute-start | bytes 983048 | tf_op jit(solution)/shard_map/ppermute | solution.py:315
  33.7 1.6 %collective-permute-done.10.refs_2_ = bf16[2,640,128]{2,1,0:T(8,128)(2,1)S(1)} collective-permute-done((bf16[2,640,128]{2,1,0:T(8,128)(2,1)S(1)}, bf16[2,640,128]{2,1,0:T(8,128)(2,1)S(1)}, u32[]{:S(2)}, u32[]{:S(2)}) %collective-permute-start.10) | collective-permute-done | bytes 327712 | tf_op jit(solution)/shard_map/ppermute | solution.py:315
  35.3 3.1 %project_640.7 = (bf16[640,128]{1,0:T(8,128)(2,1)S(1)}, bf16[640,128]{1,0:T(8,128)(2,1)S(1)}, bf16[2,640,128]{2,1,0:T(8,128)(2,1)S(1)}, bf16[2,640,128]{2,1,0:T(...) custom-call(bf16[512,2048]{1,0:T(8,128)(2,1)S(1)} %get-tuple-element.94.masked_ref, ...), custom_call_target="tpu_custom_call" | custom-call | flops 1000 | bytes 1000 | tf_op jit(solution)/shard_map/project_640/pallas_call | solution.py:192
  38.4 0.1 collective-permute-start.11
  38.5 0.5 collective-permute-start.12
  39.0 0.9 %collective-permute-done.11.gate_ref = bf16[640,128]{1,0:T(8,128)(2,1)S(1)} collective-permute-done((bf16[640,128]{1,0:T(8,128)(2,1)S(1)}, bf16[640,128]{1,0:T(8,128)(2,1)S(1)}, u32[]{:S(2)}, u32[]{:S(2)}) %collective-permute-start.11) | collective-permute-done | bytes 163872 | tf_op jit(solution)/shard_map/ppermute | solution.py:308
  39.9 0.2 collective-permute-done.12.up_ref
  40.1 0.1 add_1280.1
  40.2 0.5 collective-permute-start.16
  40.7 1.5 %collective-permute-done.13.refs_2_ = bf16[2,640,128]{2,1,0:T(8,128)(2,1)S(1)} collective-permute-done((bf16[2,640,128]{2,1,0:T(8,128)(2,1)S(1)}, bf16[2,640,128]{2,1,0:T(8,128)(2,1)S(1)}, u32[]{:S(2)}, u32[]{:S(2)}) %collective-permute-start.13) | collective-permute-done | bytes 327712 | tf_op jit(solution)/shard_map/ppermute | solution.py:315
  42.2 3.1 %project_640.8 = (bf16[640,128]{1,0:T(8,128)(2,1)S(1)}, bf16[640,128]{1,0:T(8,128)(2,1)S(1)}, bf16[2,640,128]{2,1,0:T(8,128)(2,1)S(1)}, bf16[2,640,128]{2,1,0:T(...) custom-call(bf16[512,2048]{1,0:T(8,128)(2,1)S(1)} %get-tuple-element.94.masked_ref, ...), custom_call_target="tpu_custom_call" | custom-call | flops 1000 | bytes 1000 | tf_op jit(solution)/shard_map/project_640/pallas_call | solution.py:192
  45.4 0.1 collective-permute-start.14
  45.4 0.5 collective-permute-start.15
  45.9 0.9 %collective-permute-done.14.gate_ref = bf16[640,128]{1,0:T(8,128)(2,1)S(1)} collective-permute-done((bf16[640,128]{1,0:T(8,128)(2,1)S(1)}, bf16[640,128]{1,0:T(8,128)(2,1)S(1)}, u32[]{:S(2)}, u32[]{:S(2)}) %collective-permute-start.14) | collective-permute-done | bytes 163872 | tf_op jit(solution)/shard_map/ppermute | solution.py:308
  46.8 0.2 collective-permute-done.15.up_ref
  47.0 0.1 add_1920.1
  47.1 1.4 %collective-permute-start.17 = (bf16[2,640,128]{2,1,0:T(8,128)(2,1)S(1)}, bf16[2,640,128]{2,1,0:T(8,128)(2,1)S(1)}, u32[]{:S(2)}, u32[]{:S(2)}) collective-permute-start(bf16[2,640,128]{2,1,0:T(8,128)(2,1)S(1)} %add_1920.1), channel_id=1, source_target_pairs={{0,2},{1,3},{2,0},{3,1},{4,6},{5,7},{6,4},{7,5},{8,10},{9,11},{10,... | collective-permute-start | bytes 983048 | tf_op jit(solution)/shard_map/ppermute | solution.py:315
  48.5 0.5 collective-permute-start.26
  49.1 1.1 %collective-permute-done.16.refs_2_ = bf16[2,640,128]{2,1,0:T(8,128)(2,1)S(1)} collective-permute-done((bf16[2,640,128]{2,1,0:T(8,128)(2,1)S(1)}, bf16[2,640,128]{2,1,0:T(8,128)(2,1)S(1)}, u32[]{:S(2)}, u32[]{:S(2)}) %collective-permute-start.16) | collective-permute-done | bytes 327712 | tf_op jit(solution)/shard_map/ppermute | solution.py:315
  50.2 3.1 %project_640.9 = (bf16[640,128]{1,0:T(8,128)(2,1)S(1)}, bf16[640,128]{1,0:T(8,128)(2,1)S(1)}, bf16[2,640,128]{2,1,0:T(8,128)(2,1)S(1)}, bf16[2,640,128]{2,1,0:T(8,128)(2,1)S(1)}, bf16[2,640,128]{2,1,0:T(8,128)(2,1)S(1)}) custom-call(bf16[512,2048]{1,0:T(8,128)(2,1)S(1)} %get-tuple-element.94.masked_ref, ...), custom_call_target="tpu_custom_call" | custom-call | flops 1000 | bytes 1000 | tf_op jit(solution)/shard_map/project_640/pallas_call | solution.py:192
  53.3 0.1 collective-permute-start.19
  53.3 0.5 collective-permute-start.20
  53.8 0.9 %collective-permute-done.19.gate_ref = bf16[640,128]{1,0:T(8,128)(2,1)S(1)} collective-permute-done((bf16[640,128]{1,0:T(8,128)(2,1)S(1)}, bf16[640,128]{1,0:T(8,128)(2,1)S(1)}, u32[]{:S(2)}, u32[]{:S(2)}) %collective-permute-start.19) | collective-permute-done | bytes 163872 | tf_op jit(solution)/shard_map/ppermute | solution.py:308
  54.7 0.1 collective-permute-start.24
  54.9 0.1 collective-permute-done.20.up_ref
  55.0 0.3 collective-permute-start.23
  55.2 0.1 add_2560.1
  55.3 1.8 %collective-permute-done.17.refs_2_ = bf16[2,640,128]{2,1,0:T(8,128)(2,1)S(1)} collective-permute-done((bf16[2,640,128]{2,1,0:T(8,128)(2,1)S(1)}, bf16[2,640,128]{2,1,0:T(8,128)(2,1)S(1)}, u32[]{:S(2)}, u32[]{:S(2)}) %collective-permute-start.17) | collective-permute-done | bytes 327712 | tf_op jit(solution)/shard_map/ppermute | solution.py:315
  57.2 1.3 %collective-permute-start.21 = (bf16[2,640,128]{2,1,0:T(8,128)(2,1)S(1)}, bf16[2,640,128]{2,1,0:T(8,128)(2,1)S(1)}, u32[]{:S(2)}, u32[]{:S(2)}) collective-permute-start(bf16[2,640,128]{2,1,0:T(8,128)(2,1)S(1)} %add_2560.1), channel_id=1, source_target_pairs={{0,2},{1,3},{2,0},{3,1},{4,6},{5,7},{6,4},{7,5},{8,10},{9,11},{10,... | collective-permute-start | bytes 983048 | tf_op jit(solution)/shard_map/ppermute | solution.py:315
  58.4 0.2 collective-permute-start.18
  58.7 0.9 %swiglu_5.1.refs_3_ = bf16[8,16,3696]{2,1,0:T(8,128)(2,1)} custom-call(bf16[2,496,128]{2,1,0:T(8,128)(2,1)S(1)} %get-tuple-element.116.refs_0_, bf16[2,496,128]{2,1,0:T(8,128)(2,1)S(1)} %collective-permute-done.26.refs_1_, bf16[2,496,128]{2,1,0:T(8,128)(2,1)S(1)} %collective-permute-done.7.refs_2_), custom_call_target="tpu_custom_call" | custom-call | flops 1000 | bytes 1000 | tf_op jit(solution)/shard_map/swiglu_5/pallas_call | solution.py:253
  59.6 0.9 %swiglu_0.1.refs_3_ = bf16[8,16,3696]{2,1,0:T(8,128)(2,1)} custom-call(bf16[2,640,128]{2,1,0:T(8,128)(2,1)S(1)} %get-tuple-element.113.refs_0_, bf16[2,640,128]{2,1,0:T(8,128)(2,1)S(1)} %collective-permute-done.25.refs_1_, bf16[2,640,128]{2,1,0:T(8,128)(2,1)S(1)} %collective-permute-done.10.refs_2_, ...), custom_call_target="tpu_custom_call", output_to_operand_aliasing={{}: (3, {})} | custom-call | flops 1000 | bytes 1000 | tf_op jit(solution)/shard_map/swiglu_0/pallas_call | solution.py:253
  60.6 0.9 %swiglu_1.1.refs_3_ = bf16[8,16,3696]{2,1,0:T(8,128)(2,1)} custom-call(bf16[2,640,128]{2,1,0:T(8,128)(2,1)S(1)} %get-tuple-element.110.refs_0_, bf16[2,640,128]{2,1,0:T(8,128)(2,1)S(1)} %collective-permute-done.24.refs_1_, bf16[2,640,128]{2,1,0:T(8,128)(2,1)S(1)} %collective-permute-done.13.refs_2_, ...), custom_call_target="tpu_custom_call", output_to_operand_aliasing={{}: (3, {})} | custom-call | flops 1000 | bytes 1000 | tf_op jit(solution)/shard_map/swiglu_1/pallas_call | solution.py:253
  61.5 0.9 %swiglu_2.1.refs_3_ = bf16[8,16,3696]{2,1,0:T(8,128)(2,1)} custom-call(bf16[2,640,128]{2,1,0:T(8,128)(2,1)S(1)} %get-tuple-element.107.refs_0_, bf16[2,640,128]{2,1,0:T(8,128)(2,1)S(1)} %collective-permute-done.23.refs_1_, bf16[2,640,128]{2,1,0:T(8,128)(2,1)S(1)} %collective-permute-done.16.refs_2_, ...), custom_call_target="tpu_custom_call", output_to_operand_aliasing={{}: (3, {})} | custom-call | flops 1000 | bytes 1000 | tf_op jit(solution)/shard_map/swiglu_2/pallas_call | solution.py:253
  62.4 0.9 %swiglu_3.1.refs_3_ = bf16[8,16,3696]{2,1,0:T(8,128)(2,1)} custom-call(bf16[2,640,128]{2,1,0:T(8,128)(2,1)S(1)} %get-tuple-element.104.refs_0_, bf16[2,640,128]{2,1,0:T(8,128)(2,1)S(1)} %collective-permute-done.22.refs_1_, bf16[2,640,128]{2,1,0:T(8,128)(2,1)S(1)} %collective-permute-done.17.refs_2_, ...), custom_call_target="tpu_custom_call", output_to_operand_aliasing={{}: (3, {})} | custom-call | flops 1000 | bytes 1000 | tf_op jit(solution)/shard_map/swiglu_3/pallas_call | solution.py:253
  63.4 3.9 %collective-permute-done.21.refs_2_ = bf16[2,640,128]{2,1,0:T(8,128)(2,1)S(1)} collective-permute-done((bf16[2,640,128]{2,1,0:T(8,128)(2,1)S(1)}, bf16[2,640,128]{2,1,0:T(8,128)(2,1)S(1)}, u32[]{:S(2)}, u32[]{:S(2)}) %collective-permute-start.21) | collective-permute-done | bytes 327712 | tf_op jit(solution)/shard_map/ppermute | solution.py:315
  67.3 0.9 %swiglu_4.1 = bf16[8,16,3696]{2,1,0:T(8,128)(2,1)} custom-call(bf16[2,640,128]{2,1,0:T(8,128)(2,1)S(1)} %get-tuple-element.96.refs_0_, bf16[2,640,128]{2,1,0:T(8,128)(2,1)S(1)} %collective-permute-done.18.refs_1_, bf16[2,640,128]{2,1,0:T(8,128)(2,1)S(1)} %collective-permute-done.21.refs_2_, ...), custom_call_target="tpu_custom_call", output_to_operand_aliasing={{}: (3, {})} | custom-call | flops 1000 | bytes 1000 | tf_op jit(solution)/shard_map/swiglu_4/pallas_call | solution.py:253
  (12 shorter events, 0.0 us)
Async XLA Ops:
  0.0 11.9 %copy-start = (bf16[16,2048]{1,0:T(8,128)(2,1)S(1)}, bf16[16,2048]{1,0:T(8,128)(2,1)}, u32[]{:S(2)}) copy-start(bf16[16,2048]{1,0:T(8,128)(2,1)} %refs_0_.1) | copy-start | bytes 196612
  0.0 8.5 %collective-permute-start.1 = (bf16[16,2048]{1,0:T(8,128)(2,1)}, bf16[16,2048]{1,0:T(8,128)(2,1)S(1)}, u32[]{:S(2)}, u32[]{:S(2)}) collective-permute-start(bf16[16,2048]{1,0:T(8,128)(2,1)} %refs_0_.1), channel_id=1, source_target_pairs={{0,8},{4,12},{8,0},{12,4},{1,9},{5,13},{9,1},{13,5},{2,10},{6,14},... | collective-permute-start | bytes 196616 | tf_op jit(solution)/shard_map/ppermute | solution.py:283
  4.0 4.5 %collective-permute-start = (bf16[16,2048]{1,0:T(8,128)(2,1)}, bf16[16,2048]{1,0:T(8,128)(2,1)S(1)}, u32[]{:S(2)}, u32[]{:S(2)}) collective-permute-start(bf16[16,2048]{1,0:T(8,128)(2,1)} %refs_0_.1), channel_id=1, source_target_pairs={{0,4},{4,0},{8,12},{12,8},{1,5},{5,1},{9,13},{13,9},{2,6},{6,2},{1... | collective-permute-start | bytes 196616 | tf_op jit(solution)/shard_map/ppermute | solution.py:283
  5.6 6.3 %collective-permute-start.2 = (bf16[16,2048]{1,0:T(8,128)(2,1)}, bf16[16,2048]{1,0:T(8,128)(2,1)S(1)}, u32[]{:S(2)}, u32[]{:S(2)}) collective-permute-start(bf16[16,2048]{1,0:T(8,128)(2,1)} %refs_0_.1), channel_id=1, source_target_pairs={{0,12},{4,8},{8,4},{12,0},{1,13},{5,9},{9,5},{13,1},{2,14},{6,10},... | collective-permute-start | bytes 196616 | tf_op jit(solution)/shard_map/ppermute | solution.py:283
  17.1 1.4 %collective-permute-start.3 = (bf16[496,128]{1,0:T(8,128)(2,1)S(1)}, bf16[496,128]{1,0:T(8,128)(2,1)S(1)}, u32[]{:S(2)}, u32[]{:S(2)}) collective-permute-start(bf16[496,128]{1,0:T(8,128)(2,1)S(1)} %get-tuple-element.64), channel_id=1, source_target_pairs={{0,1},{1,0},{2,3},{3,2},{4,5},{5,4},{6,7},{7,6},{8,9},{9,8},{10,11... | collective-permute-start | bytes 380936 | tf_op jit(solution)/shard_map/ppermute | solution.py:308
  17.2 1.5 %collective-permute-start.4 = (bf16[496,128]{1,0:T(8,128)(2,1)S(1)}, bf16[496,128]{1,0:T(8,128)(2,1)S(1)}, u32[]{:S(2)}, u32[]{:S(2)}) collective-permute-start(bf16[496,128]{1,0:T(8,128)(2,1)S(1)} %get-tuple-element.65), channel_id=1, source_target_pairs={{0,1},{1,0},{2,3},{3,2},{4,5},{5,4},{6,7},{7,6},{8,9},{9,8},{10,11... | collective-permute-start | bytes 380936 | tf_op jit(solution)/shard_map/ppermute | solution.py:309
  18.7 8.4 %collective-permute-start.7 = (bf16[2,496,128]{2,1,0:T(8,128)(2,1)S(1)}, bf16[2,496,128]{2,1,0:T(8,128)(2,1)S(1)}, u32[]{:S(2)}, u32[]{:S(2)}) collective-permute-start(bf16[2,496,128]{2,1,0:T(8,128)(2,1)S(1)} %add_3200.1), channel_id=1, source_target_pairs={{0,2},{1,3},{2,0},{3,1},{4,6},{5,7},{6,4},{7,5},{8,10},{9,11},{10,... | collective-permute-start | bytes 761864 | tf_op jit(solution)/shard_map/ppermute | solution.py:315
  23.4 1.5 %collective-permute-start.5 = (bf16[640,128]{1,0:T(8,128)(2,1)S(1)}, bf16[640,128]{1,0:T(8,128)(2,1)S(1)}, u32[]{:S(2)}, u32[]{:S(2)}) collective-permute-start(bf16[640,128]{1,0:T(8,128)(2,1)S(1)} %get-tuple-element.69), channel_id=1, source_target_pairs={{0,1},{1,0},{2,3},{3,2},{4,5},{5,4},{6,7},{7,6},{8,9},{9,8},{10,11... | collective-permute-start | bytes 491528 | tf_op jit(solution)/shard_map/ppermute | solution.py:308
  23.6 1.6 %collective-permute-start.6 = (bf16[640,128]{1,0:T(8,128)(2,1)S(1)}, bf16[640,128]{1,0:T(8,128)(2,1)S(1)}, u32[]{:S(2)}, u32[]{:S(2)}) collective-permute-start(bf16[640,128]{1,0:T(8,128)(2,1)S(1)} %get-tuple-element.70), channel_id=1, source_target_pairs={{0,1},{1,0},{2,3},{3,2},{4,5},{5,4},{6,7},{7,6},{8,9},{9,8},{10,11... | collective-permute-start | bytes 491528 | tf_op jit(solution)/shard_map/ppermute | solution.py:309
  25.2 10.0 %collective-permute-start.10 = (bf16[2,640,128]{2,1,0:T(8,128)(2,1)S(1)}, bf16[2,640,128]{2,1,0:T(8,128)(2,1)S(1)}, u32[]{:S(2)}, u32[]{:S(2)}) collective-permute-start(bf16[2,640,128]{2,1,0:T(8,128)(2,1)S(1)} %add_0.1), channel_id=1, source_target_pairs={{0,2},{1,3},{2,0},{3,1},{4,6},{5,7},{6,4},{7,5},{8,10},{9,11},{10,... | collective-permute-start | bytes 983048 | tf_op jit(solution)/shard_map/ppermute | solution.py:315
  30.3 1.5 %collective-permute-start.8 = (bf16[640,128]{1,0:T(8,128)(2,1)S(1)}, bf16[640,128]{1,0:T(8,128)(2,1)S(1)}, u32[]{:S(2)}, u32[]{:S(2)}) collective-permute-start(bf16[640,128]{1,0:T(8,128)(2,1)S(1)} %get-tuple-element.76), channel_id=1, source_target_pairs={{0,1},{1,0},{2,3},{3,2},{4,5},{5,4},{6,7},{7,6},{8,9},{9,8},{10,11... | collective-permute-start | bytes 491528 | tf_op jit(solution)/shard_map/ppermute | solution.py:308
  30.4 1.6 %collective-permute-start.9 = (bf16[640,128]{1,0:T(8,128)(2,1)S(1)}, bf16[640,128]{1,0:T(8,128)(2,1)S(1)}, u32[]{:S(2)}, u32[]{:S(2)}) collective-permute-start(bf16[640,128]{1,0:T(8,128)(2,1)S(1)} %get-tuple-element.77), channel_id=1, source_target_pairs={{0,1},{1,0},{2,3},{3,2},{4,5},{5,4},{6,7},{7,6},{8,9},{9,8},{10,11... | collective-permute-start | bytes 491528 | tf_op jit(solution)/shard_map/ppermute | solution.py:309
  32.1 10.1 %collective-permute-start.13 = (bf16[2,640,128]{2,1,0:T(8,128)(2,1)S(1)}, bf16[2,640,128]{2,1,0:T(8,128)(2,1)S(1)}, u32[]{:S(2)}, u32[]{:S(2)}) collective-permute-start(bf16[2,640,128]{2,1,0:T(8,128)(2,1)S(1)} %add_640.1), channel_id=1, source_target_pairs={{0,2},{1,3},{2,0},{3,1},{4,6},{5,7},{6,4},{7,5},{8,10},{9,11},{10,... | collective-permute-start | bytes 983048 | tf_op jit(solution)/shard_map/ppermute | solution.py:315
  38.4 1.5 %collective-permute-start.11 = (bf16[640,128]{1,0:T(8,128)(2,1)S(1)}, bf16[640,128]{1,0:T(8,128)(2,1)S(1)}, u32[]{:S(2)}, u32[]{:S(2)}) collective-permute-start(bf16[640,128]{1,0:T(8,128)(2,1)S(1)} %get-tuple-element.83), channel_id=1, source_target_pairs={{0,1},{1,0},{2,3},{3,2},{4,5},{5,4},{6,7},{7,6},{8,9},{9,8},{10,11... | collective-permute-start | bytes 491528 | tf_op jit(solution)/shard_map/ppermute | solution.py:308
  38.5 1.6 %collective-permute-start.12 = (bf16[640,128]{1,0:T(8,128)(2,1)S(1)}, bf16[640,128]{1,0:T(8,128)(2,1)S(1)}, u32[]{:S(2)}, u32[]{:S(2)}) collective-permute-start(bf16[640,128]{1,0:T(8,128)(2,1)S(1)} %get-tuple-element.84), channel_id=1, source_target_pairs={{0,1},{1,0},{2,3},{3,2},{4,5},{5,4},{6,7},{7,6},{8,9},{9,8},{10,11... | collective-permute-start | bytes 491528 | tf_op jit(solution)/shard_map/ppermute | solution.py:309
  40.2 10.0 %collective-permute-start.16 = (bf16[2,640,128]{2,1,0:T(8,128)(2,1)S(1)}, bf16[2,640,128]{2,1,0:T(8,128)(2,1)S(1)}, u32[]{:S(2)}, u32[]{:S(2)}) collective-permute-start(bf16[2,640,128]{2,1,0:T(8,128)(2,1)S(1)} %add_1280.1), channel_id=1, source_target_pairs={{0,2},{1,3},{2,0},{3,1},{4,6},{5,7},{6,4},{7,5},{8,10},{9,11},{10,... | collective-permute-start | bytes 983048 | tf_op jit(solution)/shard_map/ppermute | solution.py:315
  45.4 1.5 %collective-permute-start.14 = (bf16[640,128]{1,0:T(8,128)(2,1)S(1)}, bf16[640,128]{1,0:T(8,128)(2,1)S(1)}, u32[]{:S(2)}, u32[]{:S(2)}) collective-permute-start(bf16[640,128]{1,0:T(8,128)(2,1)S(1)} %get-tuple-element.90), channel_id=1, source_target_pairs={{0,1},{1,0},{2,3},{3,2},{4,5},{5,4},{6,7},{7,6},{8,9},{9,8},{10,11... | collective-permute-start | bytes 491528 | tf_op jit(solution)/shard_map/ppermute | solution.py:308
  45.4 1.6 %collective-permute-start.15 = (bf16[640,128]{1,0:T(8,128)(2,1)S(1)}, bf16[640,128]{1,0:T(8,128)(2,1)S(1)}, u32[]{:S(2)}, u32[]{:S(2)}) collective-permute-start(bf16[640,128]{1,0:T(8,128)(2,1)S(1)} %get-tuple-element.91), channel_id=1, source_target_pairs={{0,1},{1,0},{2,3},{3,2},{4,5},{5,4},{6,7},{7,6},{8,9},{9,8},{10,11... | collective-permute-start | bytes 491528 | tf_op jit(solution)/shard_map/ppermute | solution.py:309
  47.1 10.0 %collective-permute-start.17 = (bf16[2,640,128]{2,1,0:T(8,128)(2,1)S(1)}, bf16[2,640,128]{2,1,0:T(8,128)(2,1)S(1)}, u32[]{:S(2)}, u32[]{:S(2)}) collective-permute-start(bf16[2,640,128]{2,1,0:T(8,128)(2,1)S(1)} %add_1920.1), channel_id=1, source_target_pairs={{0,2},{1,3},{2,0},{3,1},{4,6},{5,7},{6,4},{7,5},{8,10},{9,11},{10,... | collective-permute-start | bytes 983048 | tf_op jit(solution)/shard_map/ppermute | solution.py:315
  48.5 9.9 %collective-permute-start.25 = (bf16[2,640,128]{2,1,0:T(8,128)(2,1)S(1)}, bf16[2,640,128]{2,1,0:T(8,128)(2,1)S(1)}, u32[]{:S(2)}, u32[]{:S(2)}) collective-permute-start(bf16[2,640,128]{2,1,0:T(8,128)(2,1)S(1)} %get-tuple-element.114), channel_id=1, source_target_pairs={{0,1},{1,0},{2,3},{3,2},{4,5},{5,4},{6,7},{7,6},{8,9},{9,8},{10,11... | collective-permute-start | bytes 983048 | tf_op jit(solution)/shard_map/ppermute | solution.py:312
  48.5 8.6 %collective-permute-start.26 = (bf16[2,496,128]{2,1,0:T(8,128)(2,1)S(1)}, bf16[2,496,128]{2,1,0:T(8,128)(2,1)S(1)}, u32[]{:S(2)}, u32[]{:S(2)}) collective-permute-start(bf16[2,496,128]{2,1,0:T(8,128)(2,1)S(1)} %get-tuple-element.117), channel_id=1, source_target_pairs={{0,1},{1,0},{2,3},{3,2},{4,5},{5,4},{6,7},{7,6},{8,9},{9,8},{10,11... | collective-permute-start | bytes 761864 | tf_op jit(solution)/shard_map/ppermute | solution.py:312
  53.3 1.5 %collective-permute-start.19 = (bf16[640,128]{1,0:T(8,128)(2,1)S(1)}, bf16[640,128]{1,0:T(8,128)(2,1)S(1)}, u32[]{:S(2)}, u32[]{:S(2)}) collective-permute-start(bf16[640,128]{1,0:T(8,128)(2,1)S(1)} %get-tuple-element.101), channel_id=1, source_target_pairs={{0,1},{1,0},{2,3},{3,2},{4,5},{5,4},{6,7},{7,6},{8,9},{9,8},{10,11... | collective-permute-start | bytes 491528 | tf_op jit(solution)/shard_map/ppermute | solution.py:308
  53.3 1.6 %collective-permute-start.20 = (bf16[640,128]{1,0:T(8,128)(2,1)S(1)}, bf16[640,128]{1,0:T(8,128)(2,1)S(1)}, u32[]{:S(2)}, u32[]{:S(2)}) collective-permute-start(bf16[640,128]{1,0:T(8,128)(2,1)S(1)} %get-tuple-element.102), channel_id=1, source_target_pairs={{0,1},{1,0},{2,3},{3,2},{4,5},{5,4},{6,7},{7,6},{8,9},{9,8},{10,11... | collective-permute-start | bytes 491528 | tf_op jit(solution)/shard_map/ppermute | solution.py:309
  54.7 5.8 %collective-permute-start.24 = (bf16[2,640,128]{2,1,0:T(8,128)(2,1)S(1)}, bf16[2,640,128]{2,1,0:T(8,128)(2,1)S(1)}, u32[]{:S(2)}, u32[]{:S(2)}) collective-permute-start(bf16[2,640,128]{2,1,0:T(8,128)(2,1)S(1)} %get-tuple-element.111), channel_id=1, source_target_pairs={{0,1},{1,0},{2,3},{3,2},{4,5},{5,4},{6,7},{7,6},{8,9},{9,8},{10,11... | collective-permute-start | bytes 983048 | tf_op jit(solution)/shard_map/ppermute | solution.py:312
  55.0 6.5 %collective-permute-start.23 = (bf16[2,640,128]{2,1,0:T(8,128)(2,1)S(1)}, bf16[2,640,128]{2,1,0:T(8,128)(2,1)S(1)}, u32[]{:S(2)}, u32[]{:S(2)}) collective-permute-start(bf16[2,640,128]{2,1,0:T(8,128)(2,1)S(1)} %get-tuple-element.108), channel_id=1, source_target_pairs={{0,1},{1,0},{2,3},{3,2},{4,5},{5,4},{6,7},{7,6},{8,9},{9,8},{10,11... | collective-permute-start | bytes 983048 | tf_op jit(solution)/shard_map/ppermute | solution.py:312
  57.2 5.3 %collective-permute-start.22 = (bf16[2,640,128]{2,1,0:T(8,128)(2,1)S(1)}, bf16[2,640,128]{2,1,0:T(8,128)(2,1)S(1)}, u32[]{:S(2)}, u32[]{:S(2)}) collective-permute-start(bf16[2,640,128]{2,1,0:T(8,128)(2,1)S(1)} %get-tuple-element.105), channel_id=1, source_target_pairs={{0,1},{1,0},{2,3},{3,2},{4,5},{5,4},{6,7},{7,6},{8,9},{9,8},{10,11... | collective-permute-start | bytes 983048 | tf_op jit(solution)/shard_map/ppermute | solution.py:312
  57.2 10.1 %collective-permute-start.21 = (bf16[2,640,128]{2,1,0:T(8,128)(2,1)S(1)}, bf16[2,640,128]{2,1,0:T(8,128)(2,1)S(1)}, u32[]{:S(2)}, u32[]{:S(2)}) collective-permute-start(bf16[2,640,128]{2,1,0:T(8,128)(2,1)S(1)} %add_2560.1), channel_id=1, source_target_pairs={{0,2},{1,3},{2,0},{3,1},{4,6},{5,7},{6,4},{7,5},{8,10},{9,11},{10,... | collective-permute-start | bytes 983048 | tf_op jit(solution)/shard_map/ppermute | solution.py:315
  58.4 8.9 %collective-permute-start.18 = (bf16[2,640,128]{2,1,0:T(8,128)(2,1)S(1)}, bf16[2,640,128]{2,1,0:T(8,128)(2,1)S(1)}, u32[]{:S(2)}, u32[]{:S(2)}) collective-permute-start(bf16[2,640,128]{2,1,0:T(8,128)(2,1)S(1)} %get-tuple-element.99), channel_id=1, source_target_pairs={{0,1},{1,0},{2,3},{3,2},{4,5},{5,4},{6,7},{7,6},{8,9},{9,8},{10,11... | collective-permute-start | bytes 983048 | tf_op jit(solution)/shard_map/ppermute | solution.py:312
